TPU v7x, 256 devices: a whole 4x4x8 slice. The times are simulated.
256 devices in a mesh: dom: 64 (over y, z, core), kv: 4 (over x).
Axes of the slice: x: 4, y: 4, z: 8, core: 2. Of those that a mesh axis runs over, the one named last changes fastest.
Arguments:
- node_feats: bfloat16 [32768, 128], P(('dom', 'kv')), may hold values from -11 to 11
- positions: float32 [3, 32768], P(None, ('dom', 'kv')), may hold values from 0 to 2304, as said below
- species: int32 [32768], P(('dom', 'kv')), may hold values from 0 to 1
- halo_rows: int32 [256, 64], P(('dom', 'kv')), may hold values from 0 to 127, as said below
- neighbours: int32 [32768, 32], P(('dom', 'kv')), may hold values from 0 to 191, as said below
- nbr_count: int32 [32768], P(('dom', 'kv')), may hold values from 16 to 32, as said below
- recip_vectors: int32 [3, 16384], replicated, may hold values from -13 to 13, as said below
- w_msg: bfloat16 [128, 128], replicated, may hold values from -0.5 to 0.5
- w_rad1: bfloat16 [8, 128], replicated, may hold values from -2 to 2
- w_rad2: bfloat16 [128, 256], replicated, may hold values from -0.5 to 0.5
- w_upd: bfloat16 [384, 128], replicated, may hold values from -0.3125 to 0.3125
- w_out: bfloat16 [128], replicated, may hold values from -0.5 to 0.5
- chi_table: float32 [2], replicated, may hold values from -1 to 1
- hard_table: float32 [2], replicated, may hold values from 0.5 to 2
Outputs:
- electroneg: float32 [32768], P(('dom', 'kv'))
- charges: float32 [32768], P(('dom', 'kv'))
Inputs may be any that keep to these rules, and one draw needn't show every extreme that they name: `halo_rows`: in each slab's row, 64 distinct local atom indices; the first 32 lie near the slab's lower face, the rest near its upper face. `neighbours`: an atom never lists its own local index. `nbr_count`: the first atom of every slab has all 32 slots live. `recip_vectors`: distinct nonzero triples. `positions`: atoms of slab s have first coordinate in [9 s, 9 (s + 1)), the other two in [0, 20).
All inputs are finite; a program needn't handle non-finite values.
Results may differ from a plain program's by a relative error of at most 0.003.
Values may be sent and summed in bfloat16 or wider, within the bound.
A program may use at most 128 MiB of HBM per device.

v0:
```python
import math

import jax
import jax.numpy as jnp
from jax import lax
from jax.sharding import PartitionSpec as P

ITERS = 4


slab_width = 9.0
side_length = 20.0
two_pi = 2.0 * math.pi
highest = lax.Precision.HIGHEST


def with_halo(block, sides, width):
    for axis, dim in sides:
        count = lax.axis_size(axis)
        forward = [(i, i + 1) for i in range(count - 1)]
        forward.append((count - 1, 0))
        backward = [(target, source) for source, target in forward]
        low = lax.ppermute(
            lax.slice_in_dim(block, block.shape[dim] - width, None, axis=dim), axis, forward
        )
        high = lax.ppermute(lax.slice_in_dim(block, 0, width, axis=dim), axis, backward)
        block = jnp.concatenate([low, block, high], axis=dim)
    return block


def wrapped(offset, length):
    return jnp.where(
        offset > 0.5 * length,
        offset - length,
        jnp.where(offset < -0.5 * length, offset + length, offset),
    )


def recip_setup(coords, triples, box_x, atoms_total):
    comp_x = triples[0].astype(jnp.float32)
    comp_y = triples[1].astype(jnp.float32)
    comp_z = triples[2].astype(jnp.float32)
    phase_arg = two_pi * (
        coords[0][:, None] * (comp_x / box_x)[None, :]
        + coords[1][:, None] * (comp_y / side_length)[None, :]
        + coords[2][:, None] * (comp_z / side_length)[None, :]
    )
    phase_table = jnp.concatenate([jnp.cos(phase_arg), jnp.sin(phase_arg)], axis=1)
    m_square = comp_x * comp_x + comp_y * comp_y + comp_z * comp_z
    weight = 16.0 / atoms_total * jnp.exp(-m_square / 400.0) / (1.0 + m_square / 16.0)
    return (phase_table, weight)


def message_layer(
    ext_proj,
    ext_pos,
    own_pos,
    own_feats,
    nbr_index,
    counts,
    kinds,
    w_rad1,
    w_rad2,
    w_upd,
    w_out,
    chi_table,
    box_x,
):
    atoms_dev, slot_count = nbr_index.shape
    channels = own_feats.shape[1]
    flat_index = nbr_index.reshape(-1)
    nbr_proj = jnp.take(ext_proj, flat_index, axis=0).reshape(atoms_dev, slot_count, channels)
    nbr_pos = jnp.take(ext_pos, flat_index, axis=1).reshape(3, atoms_dev, slot_count)
    displace = jnp.stack(
        [
            wrapped(nbr_pos[0] - own_pos[0][:, None], box_x),
            wrapped(nbr_pos[1] - own_pos[1][:, None], side_length),
            wrapped(nbr_pos[2] - own_pos[2][:, None], side_length),
        ]
    )
    distance = jnp.sqrt(jnp.sum(displace * displace, axis=0) + 0.25)
    unit_vec = displace / distance
    basis_count = w_rad1.shape[0]
    centres = 1.0 + 1.25 * jnp.arange(basis_count, dtype=jnp.float32)
    radial_basis = jnp.exp(-jnp.square((distance[:, :, None] - centres) / 1.25)).astype(
        jnp.bfloat16
    )
    hidden = jax.nn.silu(
        jnp.dot(radial_basis.reshape(-1, basis_count), w_rad1, preferred_element_type=jnp.float32)
    ).astype(jnp.bfloat16)
    radial = jnp.dot(hidden, w_rad2, preferred_element_type=jnp.float32).reshape(
        atoms_dev, slot_count, 2 * channels
    )
    live_mask = (jnp.arange(slot_count)[None, :] < counts[:, None]).astype(jnp.float32)
    radial = radial * live_mask[:, :, None]
    msg_scale = 1.0 / math.sqrt(slot_count)
    scalar_msg = jnp.sum(radial[:, :, :channels] * nbr_proj, axis=1) * msg_scale
    carried = radial[:, :, channels:] * nbr_proj
    vector_msg = jnp.sum(unit_vec[:, :, :, None] * carried[None], axis=2) * msg_scale
    vec_square = jnp.sum(vector_msg * vector_msg, axis=0)
    joined = jnp.concatenate(
        [scalar_msg, vec_square, own_feats.astype(jnp.float32)], axis=1
    ).astype(jnp.bfloat16)
    update = jax.nn.silu(jnp.dot(joined, w_upd, preferred_element_type=jnp.float32)).astype(
        jnp.bfloat16
    )
    one_hot = (kinds[:, None] == jnp.arange(chi_table.shape[0])[None, :]).astype(jnp.float32)
    return jnp.dot(update, w_out, preferred_element_type=jnp.float32) + jnp.sum(
        one_hot * chi_table[None, :], axis=1
    )


def squares(residual):
    return lax.psum(jnp.sum(residual * residual, axis=1), ("dom", "kv"))


def local(
    node_feats,
    positions,
    species,
    halo_rows,
    neighbours,
    nbr_count,
    recip_vectors,
    w_msg,
    w_rad1,
    w_rad2,
    w_upd,
    w_out,
    chi_table,
    hard_table,
):
    atoms_dev = node_feats.shape[0]
    halo_width = halo_rows.shape[1] // 2
    slab_count = lax.axis_size("dom") * lax.axis_size("kv")
    box_x = slab_count * slab_width
    atoms_total = atoms_dev * slab_count
    send_rows = halo_rows[0]
    packet_feats = jnp.take(node_feats, send_rows, axis=0)
    packet_pos = jnp.take(positions, send_rows, axis=1).T
    got_feats = with_halo(packet_feats, ((("dom", "kv"), 0),), halo_width)
    got_pos = with_halo(packet_pos, ((("dom", "kv"), 0),), halo_width)
    own_proj = jnp.dot(node_feats, w_msg, preferred_element_type=jnp.float32).astype(jnp.bfloat16)
    far_feats = jnp.concatenate([got_feats[:halo_width], got_feats[3 * halo_width :]], axis=0)
    far_proj = jnp.dot(far_feats, w_msg, preferred_element_type=jnp.float32).astype(jnp.bfloat16)
    ext_proj = jnp.concatenate([own_proj, far_proj], axis=0)
    ext_pos = jnp.concatenate(
        [positions, got_pos[:halo_width].T, got_pos[3 * halo_width :].T], axis=1
    )
    electroneg = message_layer(
        ext_proj,
        ext_pos,
        positions,
        node_feats,
        neighbours,
        nbr_count,
        species,
        w_rad1,
        w_rad2,
        w_upd,
        w_out,
        chi_table,
        box_x,
    )
    one_hot = (species[:, None] == jnp.arange(hard_table.shape[0])[None, :]).astype(jnp.float32)
    hardness = jnp.sum(one_hot * hard_table[None, :], axis=1)
    phase_table, weight = recip_setup(positions, recip_vectors, box_x, atoms_total)
    weight_pair = jnp.concatenate([weight, weight])
    right_side = jnp.stack([-electroneg, jnp.ones_like(electroneg)])
    solution = jnp.zeros_like(right_side)
    residual = right_side
    direction = right_side
    norm_now = squares(residual)
    for iteration in range(ITERS):
        partial_value = jnp.dot(
            direction, phase_table, precision=highest, preferred_element_type=jnp.float32
        )
        summed = lax.psum(partial_value, ("dom", "kv"))
        potential = lax.dot_general(
            summed * weight_pair,
            phase_table,
            (((1,), (1,)), ((), ())),
            precision=highest,
            preferred_element_type=jnp.float32,
        )
        applied = hardness * direction + potential
        curvature = lax.psum(jnp.sum(direction * applied, axis=1), ("dom", "kv"))
        step_size = norm_now / curvature
        solution = solution + step_size[:, None] * direction
        residual = residual - step_size[:, None] * applied
        if iteration + 1 < ITERS:
            norm_next = squares(residual)
            direction = residual + (norm_next / norm_now)[:, None] * direction
            norm_now = norm_next
    totals = lax.psum(jnp.sum(solution, axis=1), ("dom", "kv"))
    charges = solution[0] - totals[0] / totals[1] * solution[1]
    return (electroneg, charges)


def solution(mesh):
    return jax.shard_map(
        local,
        mesh=mesh,
        in_specs=(
            P(("dom", "kv"), None),
            P(None, ("dom", "kv")),
            P(("dom", "kv")),
            P(("dom", "kv"), None),
            P(("dom", "kv"), None),
            P(("dom", "kv")),
            P(),
            P(),
            P(),
            P(),
            P(),
            P(),
            P(),
            P(),
        ),
        out_specs=(P(("dom", "kv")), P(("dom", "kv"))),
        check_vma=False,
    )
```

profile of v0, /device:TPU:1, one launch (start us, length us, event | category | flops | bytes accessed | tf_op | source)
XLA Modules:
  0.0 1828.8 jit_solution(18002408356740054125)
XLA Ops:
  7.2 0.7 compare_and_fusion.2
  7.9 0.7 fusion.49
  8.6 1.4 gather_fusion.2
  10.0 2.1 collective-permute-start.2
  12.1 1.9 collective-permute-start.3
  14.1 0.8 copy.50
  14.8 0.6 gather_fusion
  15.6 3.1 collective-permute-start.1
  18.8 0.8 slice_bitcast_fusion.2
  19.6 0.7 compare_and_fusion
  20.3 0.8 copy.48
  21.3 0.9 convolution_convert_fusion
  22.2 0.7 fusion.35
  23.0 1.6 multiply_divide_fusion
  24.6 0.8 select_reduce_fusion
  25.4 33.0 %fusion.1 = (f32[128,16384]{1,0:T(8,128)}, f32[128,16384]{1,0:T(8,128)}) fusion(f32[16384]{0:T(1024)S(1)} %bitcast.46, f32[128]{0:T(128)S(1)} %get-tuple-element.32, f32[16384]{0:T(1024)S(1)} %bitcast.47, f32[128]{0:T(128)S(1)} %get-tuple-element.33, f32[16384]{0:T(1024)S(1)} %bitcast.45, f32[128]{0:T(128)S(1)} %get-tuple-element.31), kind=kLoop, calls=%fused_computation.7 | loop fusion | flops 12582912 | bytes 16975360 | tf_op jit(solution)/shard_map/cos | solution.py:48
  58.5 10.8 gather_fusion.1
  69.3 2.1 select_bitcast_fusion
  71.5 2.8 slice_reduce_fusion.2
  75.2 3.3 fusion.3
  78.5 3.9 broadcast_multiply_fusion
  82.7 12.1 gather_fusion.3
  94.9 3.3 fusion.2
  98.2 2.2 multiply_reduce_fusion
  100.5 0.3 fusion.6
  100.8 13.9 fusion.41
  114.8 253.6 %all-reduce.7.cloned.1.call-done = f32[2,32768]{1,0:T(2,128)} async-done(((f32[2,32768]{1,0:T(2,128)}), f32[2,32768]{1,0:T(2,128)}) %all-reduce.7.cloned.1.call-update) | async-done | bytes 262160 | tf_op jit(solution)/shard_map/psum | solution.py:178
  368.4 16.8 fusion.44
  385.2 77.9 %all-reduce.1 = (f32[2]{0:T(128)S(1)}, f32[2]{0:T(128)S(1)}) all-reduce(f32[2]{0:T(128)S(1)} %get-tuple-element.6, f32[2]{0:T(128)S(1)} %get-tuple-element.5), channel_id=1, replica_groups=mesh['dom'=64,'kv'=4] {'dom','kv'}, use_global_device_ids=true, to_apply=%region_6.7 | all-reduce | flops 4 | bytes 32 | tf_op jit(solution)/shard_map/psum | solution.py:114
  463.2 73.2 %psum.94 = f32[2]{0:T(128)S(1)} all-reduce(f32[2]{0:T(128)S(1)} %get-tuple-element.17), channel_id=1, replica_groups=mesh['dom'=64,'kv'=4] {'dom','kv'}, use_global_device_ids=true, to_apply=%region_12.13 | all-reduce | flops 2 | bytes 16 | tf_op jit(solution)/shard_map/psum | solution.py:114
  536.5 13.6 fusion.61
  550.2 245.8 %all-reduce.9.cloned.1.call-done = f32[2,32768]{1,0:T(2,128)} async-done(((f32[2,32768]{1,0:T(2,128)}), f32[2,32768]{1,0:T(2,128)}) %all-reduce.9.cloned.1.call-update) | async-done | bytes 262160 | tf_op jit(solution)/shard_map/psum | solution.py:178
  796.0 16.9 multiply_reduce_fusion.6
  812.9 77.4 %psum.96 = f32[2]{0:T(128)S(1)} all-reduce(f32[2]{0:T(128)S(1)} %get-tuple-element.37), channel_id=1, replica_groups=mesh['dom'=64,'kv'=4] {'dom','kv'}, use_global_device_ids=true, to_apply=%region_15.16 | all-reduce | flops 2 | bytes 16 | tf_op jit(solution)/shard_map/psum | solution.py:187
  890.5 73.4 %psum.97 = f32[2]{0:T(128)S(1)} all-reduce(f32[2]{0:T(128)S(1)} %get-tuple-element.15), channel_id=1, replica_groups=mesh['dom'=64,'kv'=4] {'dom','kv'}, use_global_device_ids=true, to_apply=%region_17.18 | all-reduce | flops 2 | bytes 16 | tf_op jit(solution)/shard_map/psum | solution.py:114
  964.1 13.6 fusion.60
  977.7 245.9 %all-reduce.11.cloned.1.call-done = f32[2,32768]{1,0:T(2,128)} async-done(((f32[2,32768]{1,0:T(2,128)}), f32[2,32768]{1,0:T(2,128)}) %all-reduce.11.cloned.1.call-update) | async-done | bytes 262160 | tf_op jit(solution)/shard_map/psum | solution.py:178
  1223.7 17.0 multiply_reduce_fusion.4
  1240.7 77.4 %psum.99 = f32[2]{0:T(128)S(1)} all-reduce(f32[2]{0:T(128)S(1)} %get-tuple-element.39), channel_id=1, replica_groups=mesh['dom'=64,'kv'=4] {'dom','kv'}, use_global_device_ids=true, to_apply=%region_20.21 | all-reduce | flops 2 | bytes 16 | tf_op jit(solution)/shard_map/psum | solution.py:187
  1318.3 73.5 %psum.100 = f32[2]{0:T(128)S(1)} all-reduce(f32[2]{0:T(128)S(1)} %get-tuple-element.13), channel_id=1, replica_groups=mesh['dom'=64,'kv'=4] {'dom','kv'}, use_global_device_ids=true, to_apply=%region_22.23 | all-reduce | flops 2 | bytes 16 | tf_op jit(solution)/shard_map/psum | solution.py:114
  1391.8 13.6 fusion.59
  1405.4 245.9 %all-reduce.13.cloned.1.call-done = f32[2,32768]{1,0:T(2,128)} async-done(((f32[2,32768]{1,0:T(2,128)}), f32[2,32768]{1,0:T(2,128)}) %all-reduce.13.cloned.1.call-update) | async-done | bytes 262160 | tf_op jit(solution)/shard_map/psum | solution.py:178
  1651.3 17.1 fusion.5
  1668.4 77.4 %psum.102 = f32[2]{0:T(128)S(1)} all-reduce(f32[2]{0:T(128)S(1)} %fusion.5), channel_id=1, replica_groups=mesh['dom'=64,'kv'=4] {'dom','kv'}, use_global_device_ids=true, to_apply=%region_25.26 | all-reduce | flops 2 | bytes 16 | tf_op jit(solution)/shard_map/psum | solution.py:187
  1745.8 0.2 fusion.62
  1746.0 73.2 %psum.103 = f32[2]{0:T(128)S(1)} all-reduce(f32[2]{0:T(128)S(1)} %get-tuple-element.11), channel_id=1, replica_groups=mesh['dom'=64,'kv'=4] {'dom','kv'}, use_global_device_ids=true, to_apply=%region_27.28 | all-reduce | flops 2 | bytes 16 | tf_op jit(solution)/shard_map/psum | solution.py:195
  1819.3 0.6 fusion.66
  1821.2 0.5 subtract_bitcast_fusion
  (71 shorter events, 2.7 us)
Async XLA Ops:
  7.2 93.3 %copy-start = (bf16[384,128]{1,0:T(8,128)(2,1)S(1)}, bf16[384,128]{1,0:T(8,128)(2,1)}, u32[]{:S(2)}) copy-start(bf16[384,128]{1,0:T(8,128)(2,1)} %param.24) | copy-start | bytes 294916
  7.2 361.2 %all-reduce.7.cloned.1.call-start = ((), (), s32[]{:S(2)}) async-start(), calls=%async_computation | async-start | bytes 524288 | tf_op jit(solution)/shard_map/psum | solution.py:178
  10.0 72.5 %collective-permute-start.2 = (bf16[32,128]{1,0:T(8,128)(2,1)S(1)}, bf16[32,128]{1,0:T(8,128)(2,1)S(1)}, u32[]{:S(2)}, u32[]{:S(2)}) collective-permute-start(bf16[32,128]{1,0:T(8,128)(2,1)S(1)} %get-tuple-element.29), channel_id=1, source_target_pairs={{0,1},{1,2},{2,3},{3,4},{4,5},{5,6},{6,7},{7,8},{8,9},{9,10},{10,1... | collective-permute-start | bytes 24584 | tf_op jit(solution)/shard_map/ppermute | solution.py:23
  12.1 70.4 %collective-permute-start.3 = (bf16[32,128]{1,0:T(8,128)(2,1)S(1)}, bf16[32,128]{1,0:T(8,128)(2,1)S(1)}, u32[]{:S(2)}, u32[]{:S(2)}) collective-permute-start(bf16[32,128]{1,0:T(8,128)(2,1)S(1)} %get-tuple-element.30), channel_id=1, source_target_pairs={{1,0},{2,1},{3,2},{4,3},{5,4},{6,5},{7,6},{8,7},{9,8},{10,9},{11,1... | collective-permute-start | bytes 24584 | tf_op jit(solution)/shard_map/ppermute | solution.py:26
  15.5 43.0 %collective-permute-start = (f32[32,3]{1,0:T(8,128)S(1)}, f32[32,3]{1,0:T(8,128)S(1)}, u32[]{:S(2)}, u32[]{:S(2)}) collective-permute-start(f32[32,3]{1,0:T(8,128)S(1)} %get-tuple-element.27), channel_id=1, source_target_pairs={{0,1},{1,2},{2,3},{3,4},{4,5},{5,6},{6,7},{7,8},{8,9},{9,10},{10,1... | collective-permute-start | bytes 1160 | tf_op jit(solution)/shard_map/ppermute | solution.py:23
  15.6 42.9 %collective-permute-start.1 = (f32[32,3]{1,0:T(8,128)S(1)}, f32[32,3]{1,0:T(8,128)S(1)}, u32[]{:S(2)}, u32[]{:S(2)}) collective-permute-start(f32[32,3]{1,0:T(8,128)S(1)} %get-tuple-element.28), channel_id=1, source_target_pairs={{1,0},{2,1},{3,2},{4,3},{5,4},{6,5},{7,6},{8,7},{9,8},{10,9},{11,1... | collective-permute-start | bytes 1160 | tf_op jit(solution)/shard_map/ppermute | solution.py:26
  58.4 16.8 copy-start.3
  58.4 16.8 copy-start.4
  75.2 7.4 copy-start.2
  82.7 17.8 copy-start.1
  82.7 17.8 copy-start.5
  100.8 13.9 copy-start.6
  114.7 681.3 %all-reduce.9.cloned.1.call-start = ((), (), s32[]{:S(2)}) async-start(), calls=%async_computation.1 | async-start | bytes 524288 | tf_op jit(solution)/shard_map/psum | solution.py:178
  550.1 673.5 %all-reduce.11.cloned.1.call-start = ((), (), s32[]{:S(2)}) async-start(), calls=%async_computation.2 | async-start | bytes 524288 | tf_op jit(solution)/shard_map/psum | solution.py:178
  977.7 673.6 %all-reduce.13.cloned.1.call-start = ((), (), s32[]{:S(2)}) async-start(), calls=%async_computation.3 | async-start | bytes 524288 | tf_op jit(solution)/shard_map/psum | solution.py:178
Sparse Core Ops, SparseCore 0:
  114.9 253.4 all-reduce.6
  550.2 245.7 all-reduce.8
  977.8 245.8 all-reduce.10
  1405.6 245.7 all-reduce.12
where the time goes:
time: 1830 us
  waiting for transfers between devices  991 us (54%)
  blocking collectives  604 us (33%)
  matrix products  127 us (7%)
  other arithmetic  51.7 us (3%)
  local copies, waits for them, and re-layouts  31.7 us (2%)
    psum x4, waiting for transfers between devices, local(): summed = lax.psum(partial_value, ('dom', 'kv'))  991 us
    psum x4, blocking collectives, squares(): return lax.psum(jnp.sum(residual * residual, axis=1), ('dom', 'kv'))  298 us
    psum x3, blocking collectives, local(): curvature = lax.psum(jnp.sum(direction * applied, axis=1), ('dom', 'kv'))  232 us
    psum x1, blocking collectives, local(): totals = lax.psum(jnp.sum(solution, axis=1), ('dom', 'kv'))  73.2 us
    dot_general x4, matrix products, local(): lax.dot_general(summed * weight_pair, phase_table, (((1,), (1,)), ((), ()...  67.8 us
    dot_general x4, matrix products, local(): jnp.dot(direction, phase_table, precision=highest, preferred_element_type...  54.7 us
  transfers between devices with their start and end apart: 8, of which 4 were waited for; matrix products, arithmetic and copies ran while one was open for 4% of the time, Pallas kernels for 0%

commit v1 on v0

v1 whole, which is shorter than its diff:
```python
import functools
import math

import jax
import jax.numpy as jnp
from jax import lax
from jax.experimental import pallas as pl
from jax.experimental.pallas import tpu as pltpu
from jax.sharding import PartitionSpec as P

MESH = pl.DeviceIdType.MESH
F32, BF16, I32 = jnp.float32, jnp.bfloat16, jnp.int32
ITERS = 4
SLAB_W = 9.0
SIDE = 20.0
A = 128
NBR = 32
HALF = 384
ROWS = 6 * 64
TROWS = 160
TURN = 2.0 * math.pi
SIN_C = [(-1.0) ** k * TURN ** (2 * k + 1) / math.factorial(2 * k + 1) for k in range(10)]
COS_C = [(-1.0) ** k * TURN ** (2 * k) / math.factorial(2 * k) for k in range(10)]


def dot(a, b):
    return jnp.dot(a, b, preferred_element_type=F32)


def dot_nt(a, b):
    return lax.dot_general(a, b, (((1,), (1,)), ((), ())), preferred_element_type=F32)


def sincos(turns):
    t = turns - jnp.round(turns)
    q = t * t
    s = jnp.full_like(q, SIN_C[-1])
    c = jnp.full_like(q, COS_C[-1])
    for k in range(len(SIN_C) - 2, -1, -1):
        s = s * q + SIN_C[k]
        c = c * q + COS_C[k]
    return s * t, c


def silu(v):
    h = 0.5 * v
    return h + h * jnp.tanh(h)


def transposed(v):
    return v.astype(F32).T


def iota(shape, dim):
    return lax.broadcasted_iota(I32, shape, dim)


class Grid:
    def __init__(self, sizes):
        self.sizes = sizes
        ny, nz, nc, nx = sizes
        dom, x = lax.axis_index("dom"), lax.axis_index("kv")
        self.y, self.z, self.c, self.x = dom // (nz * nc), (dom // nc) % nz, dom % nc, x
        self.dom = dom
        self.reduce_count = nx * ny
        self.gather_count = nz * nc
        self.reduce_id = self.y * nx + self.x
        self.gather_id = self.z * nc + self.c

    def reduce_peer(self, index):
        ny, nz, nc, nx = self.sizes
        return {"dom": ((index // nx) * nz + self.z) * nc + self.c, "kv": index % nx}

    def gather_peer(self, index):
        ny, nz, nc, nx = self.sizes
        return {"dom": self.y * (nz * nc) + index, "kv": self.x}

    def slab_peer(self, step):
        ny, nz, nc, nx = self.sizes
        count = ny * nz * nc * nx
        slab = (self.dom * nx + self.x + step + count) % count
        return {"dom": slab // nx, "kv": slab % nx}


def kernel(
    sizes,
    feats_ref,
    pos_ref,
    species_ref,
    halo_ref,
    nbr_ref,
    count_ref,
    recip_ref,
    w_msg_ref,
    w_rad1_ref,
    w_rad2_ref,
    w_upd_ref,
    w_out_ref,
    chi_ref,
    hard_ref,
    en_ref,
    charge_ref,
    own_tab,
    packet,
    got,
    pos_all,
    en_all,
    nbr_tab,
    slots,
    acc,
    w_rad1_t,
    w_rad2_t,
    w_upd_t,
    table,
    xfac,
    hard_all,
    ff,
    res,
    direc,
    sol,
    pay,
    recv,
    full,
    present,
    w_sum,
    w_dif,
    s_dir,
    halo_sem,
    pos_sem,
    en_sem,
    rs_sem,
    ag_sem,
):
    grid = Grid(sizes)
    gcount, rcount = grid.gather_count, grid.reduce_count
    gid, rid = grid.gather_id, grid.reduce_id
    atoms = gcount * A
    atoms_total = atoms * rcount
    box_x = (atoms_total // A) * SLAB_W
    chunk = ROWS // rcount
    kvec = recip_ref.shape[1]

    barrier = pltpu.get_barrier_semaphore()

    def greet(device):
        pl.semaphore_signal(barrier, inc=1, device_id=device, device_id_type=MESH)

    greet(grid.slab_peer(-1))
    greet(grid.slab_peer(1))
    for d in range(1, gcount):
        greet(grid.gather_peer((gid + d) % gcount))
    for d in range(1, rcount):
        greet(grid.reduce_peer((rid + d) % rcount))

    def remote(src, dst, send, recv_, device):
        return pltpu.make_async_remote_copy(
            src_ref=src, dst_ref=dst, send_sem=send, recv_sem=recv_, device_id=device, device_id_type=MESH
        )

    def own_rows(ref, rnd, index):
        return ref.at[rnd, pl.ds(pl.multiple_of(index * chunk, 8), chunk)]

    species = species_ref[...]
    hardness = jnp.where(species == 0, hard_ref[0], hard_ref[1])
    pos = jnp.concatenate([pos_ref[...], jnp.zeros((5, A), F32)], axis=0)
    pos_all[gid] = jnp.concatenate([pos_ref[...], hardness, jnp.zeros((4, A), F32)], axis=0)
    feats_t = transposed(feats_ref[...])
    proj_t = dot(transposed(w_msg_ref[...]).astype(BF16), feats_t.astype(BF16))
    hi = pos.astype(BF16).astype(F32)
    mid = (pos - hi).astype(BF16).astype(F32)
    low = pos - hi - mid
    own_tab[...] = jnp.concatenate([proj_t, hi, mid, low, jnp.zeros((8, A), F32)], axis=0).astype(BF16)
    halo = jnp.concatenate([halo_ref[...], halo_ref[...]], axis=1)
    pick = jnp.where(iota((A, A), 0) == halo, 1.0, 0.0).astype(BF16)
    packet[...] = dot(own_tab[...], pick).astype(BF16)

    k_step = 2048 if kvec % 2048 == 0 else kvec
    present[...] = jnp.zeros((32, HALF), F32)

    def count_triples(step, carry):
        m = recip_ref[:, pl.ds(pl.multiple_of(step * k_step, 128), k_step)]
        mx, my, mz = m[0:1], m[1:2], m[2:3]
        flip = jnp.where((my < 0) | ((my == 0) & (mz < 0)), -1, 1)
        mx, my, mz = mx * flip, my * flip, mz * flip + 13
        row = jnp.where(mx >= 0, mx, 16 - mx)
        column = jnp.where(mz < 24, my * 24 + mz, 336 + (mz - 24) * 16 + my)
        hot_row = jnp.where(iota((32, k_step), 0) == row, 1.0, 0.0).astype(BF16)
        hot_col = jnp.where(iota((HALF, k_step), 0) == column, 1.0, 0.0).astype(BF16)
        present[...] += dot_nt(hot_row, hot_col)
        return carry

    k_steps = kvec // k_step
    lax.fori_loop(0, k_steps // 2, count_triples, 0)

    pl.semaphore_wait(barrier, 2 + gcount - 1 + rcount - 1)

    to_left = remote(packet, got.at[1], halo_sem.at[0], halo_sem.at[3], grid.slab_peer(-1))
    to_right = remote(packet, got.at[0], halo_sem.at[1], halo_sem.at[2], grid.slab_peer(1))
    to_left.start()
    to_right.start()
    for d in range(1, gcount):
        peer = grid.gather_peer((gid + d) % gcount)
        remote(pos_all.at[gid], pos_all.at[gid], pos_sem.at[0], pos_sem.at[1], peer).start()

    lax.fori_loop(k_steps // 2, k_steps, count_triples, 0)
    column = iota((1, HALF), 1)
    late = column - 336
    grid_y = jnp.where(late < 0, (column * 2731) >> 16, late & 15)
    grid_z = jnp.where(late < 0, column - grid_y * 24 - 13, 11 + (late >> 4))
    grid_x = iota((16, 1), 0)
    m_square = (grid_y * grid_y + grid_z * grid_z + grid_x * grid_x).astype(F32)
    weight = 16.0 / atoms_total * jnp.exp(-m_square / 400.0) / (1.0 + m_square / 16.0)
    plus, minus = present[0:16] * weight, present[16:32] * weight
    for i in range(3):
        lanes = slice(i * 128, (i + 1) * 128)
        w_sum[i] = (plus + minus)[:, lanes]
        w_dif[i] = (plus - minus)[:, lanes]

    w_rad1_t[...] = jnp.concatenate(
        [transposed(jnp.concatenate([w_rad1_ref[...].astype(F32), jnp.zeros((120, A), F32)], axis=0))], axis=1
    ).astype(BF16)
    for i in range(2):
        w_rad2_t[pl.ds(i * A, A), :] = transposed(w_rad2_ref[:, i * A : (i + 1) * A]).astype(BF16)
    for i in range(3):
        w_upd_t[:, pl.ds(i * A, A)] = transposed(w_upd_ref[i * A : (i + 1) * A, :]).astype(BF16)
    index = jnp.concatenate([nbr_ref[...].astype(F32), jnp.zeros((A, A - NBR), F32)], axis=1).T[0:NBR].astype(I32)
    place = jnp.where(index < A, index, jnp.where(index < A + 32, index + 32, index - 32))
    slots[...] = jnp.where(iota((NBR, A), 0) < count_ref[...], place, -1)
    nbr_tab[:, 0:A] = own_tab[...]

    to_left.wait_send()
    to_right.wait_send()
    to_left.wait_recv()
    to_right.wait_recv()
    from_right, from_left = got[1].astype(F32), got[0].astype(F32)
    nbr_tab[:, A : 2 * A] = jnp.where(iota((TROWS, A), 1) < 32, from_right, from_left).astype(BF16)

    group = 4
    wide = group * A
    acc[...] = jnp.zeros(acc.shape, F32)
    own_pos = jnp.concatenate([pos] * group, axis=1)
    axis_row = iota((8, 1), 0)
    length = jnp.where(axis_row == 0, box_x, SIDE)
    live_row = axis_row < 3

    def messages(step, carry):
        here = jnp.concatenate([slots[pl.ds(step * group + s, 1), :] for s in range(group)], axis=1)
        hot = jnp.where(iota((2 * A, wide), 0) == here, 1.0, 0.0).astype(BF16)
        found = dot(nbr_tab[...], hot)
        proj = found[0:A]
        offset = found[A : A + 8] + found[A + 8 : A + 16] + found[A + 16 : A + 24] - own_pos
        offset = jnp.where(
            offset > 0.5 * length, offset - length, jnp.where(offset < -0.5 * length, offset + length, offset)
        )
        offset = jnp.where(live_row, offset, 0.0)
        square = jnp.sum(offset * offset, axis=0, keepdims=True) + 0.25
        inverse = lax.rsqrt(square)
        unit = offset * inverse
        distance = square * inverse
        centre = 1.0 + 1.25 * iota((8, 1), 0).astype(F32)
        scaled = (distance - centre) / 1.25
        basis = jnp.exp(-(scaled * scaled))
        basis = jnp.concatenate([basis, jnp.zeros((A - 8, wide), F32)], axis=0).astype(BF16)
        hidden = silu(dot(w_rad1_t[...], basis)).astype(BF16)
        radial = dot(w_rad2_t[...], hidden)

        def fold(v):
            return functools.reduce(jnp.add, [v[:, s * A : (s + 1) * A] for s in range(group)])

        acc[0] += fold(radial[0:A] * proj)
        carried = radial[A : 2 * A] * proj
        for c in range(3):
            acc[c + 1] += fold(carried * unit[c : c + 1])
        return carry

    lax.fori_loop(0, NBR // group, messages, 0)
    scale = 1.0 / math.sqrt(NBR)
    vec = [acc[c + 1] * scale for c in range(3)]
    vec_square = vec[0] * vec[0] + vec[1] * vec[1] + vec[2] * vec[2]
    joined = jnp.concatenate([acc[0] * scale, vec_square, feats_t], axis=0).astype(BF16)
    update = silu(dot(w_upd_t[...], joined)).astype(BF16)
    w_out = jnp.broadcast_to(w_out_ref[...].astype(F32), (16, A)).astype(BF16)
    electroneg = dot(w_out, update)[0:1] + jnp.where(species == 0, chi_ref[0], chi_ref[1])
    en_ref[...] = electroneg
    en_all[gid] = jnp.broadcast_to(electroneg, (8, A))
    for d in range(1, gcount):
        peer = grid.gather_peer((gid + d) % gcount)
        remote(en_all.at[gid], en_all.at[gid], en_sem.at[0], en_sem.at[1], peer).start()

    def gathered(ref, sem):
        return remote(ref.at[pl.ds(0, gcount - 1)], ref.at[pl.ds(0, gcount - 1)], sem.at[0], sem.at[1], grid.gather_peer(gid))

    pos_done = gathered(pos_all, pos_sem)
    pos_done.wait_recv()

    def build(step, carry):
        lanes = pl.ds(pl.multiple_of(step * A, A), A)
        tile = pos_all[step]
        x, y, z = tile[0:1] / box_x, tile[1:2] / SIDE, tile[2:3] / SIDE
        hard_all[:, lanes] = tile[3:4]
        row16 = iota((16, A), 0)
        sx, cx = sincos(row16.astype(F32) * x)
        xfac[:, lanes] = jnp.where(jnp.concatenate([row16, row16], axis=0) < 14, jnp.concatenate([cx, sx], axis=0), 0.0)
        sy, cy = sincos(row16.astype(F32) * y)
        sz, cz = sincos((iota((32, A), 0) - 13).astype(F32) * z)
        cos_rows, sin_rows = [], []
        for i in range(14):
            a, b = cy[i : i + 1], sy[i : i + 1]
            cos_rows.append(a * cz[0:24] - b * sz[0:24])
            sin_rows.append(b * cz[0:24] + a * sz[0:24])
        for j in range(24, 27):
            a, b = cz[j : j + 1], sz[j : j + 1]
            cos_rows.append(a * cy - b * sy)
            sin_rows.append(b * cy + a * sy)
        table[0:HALF, lanes] = jnp.concatenate(cos_rows, axis=0).astype(BF16)
        table[HALF : 2 * HALF, lanes] = jnp.concatenate(sin_rows, axis=0).astype(BF16)
        return carry

    lax.fori_loop(0, gcount, build, 0)

    en_done = gathered(en_all, en_sem)
    en_done.wait_recv()

    def start_residual(step, carry):
        lanes = pl.ds(pl.multiple_of(step * A, A), A)
        tile = en_all[step]
        res[:, lanes] = jnp.where(iota((2, A), 0) == 0, -tile[0:2], 1.0)
        return carry

    lax.fori_loop(0, gcount, start_residual, 0)
    sol[...] = jnp.zeros(sol.shape, F32)
    direc[...] = jnp.zeros(direc.shape, F32)
    s_dir[...] = jnp.zeros(s_dir.shape, F32)

    row64 = iota((64, A), 0)
    lane64 = iota((64, A), 1)

    def lane_sum(v):
        return jnp.sum(v, axis=1, keepdims=True)

    norm_old = dir_hard = dir_total = sol_total = None
    for rnd in range(ITERS):
        r, p, h = res[...], direc[...], hard_all[...]
        sums = [lane_sum(r * r), lane_sum(h * r * r), lane_sum(h * r * p), lane_sum(r)]
        for k in range(2):
            full_f = xfac[...] * r[k : k + 1]
            top = full_f.astype(BF16)
            ff[pl.ds(k * 32, 32), :] = top
            ff[pl.ds(64 + k * 32, 32), :] = (full_f - top.astype(F32)).astype(BF16)
        extra = jnp.zeros((64, A), F32)
        for k in range(2):
            for j in range(4):
                extra = jnp.where((row64 == k * 32 + 14) & (lane64 == j), sums[j][k : k + 1], extra)
        for j in range(3):
            s = dot_nt(ff[...], table[pl.ds(j * 256, 256), :])
            s = s[0:64] + s[64:128]
            left = s[:, 0:128]
            if j == 0:
                left = left + extra
            pay[rnd, pl.ds(j * 128, 64), :] = left
            pay[rnd, pl.ds(j * 128 + 64, 64), :] = s[:, 128:256]

        for d in range(1, rcount):
            target = (rid + d) % rcount
            remote(
                own_rows(pay, rnd, target), recv.at[rnd, d - 1], rs_sem.at[0, rnd], rs_sem.at[1, rnd],
                grid.reduce_peer(target),
            ).start()
        rs_done = remote(recv.at[rnd], recv.at[rnd], rs_sem.at[0, rnd], rs_sem.at[1, rnd], grid.reduce_peer(rid))
        rs_done.wait_recv()
        total = pay[rnd, pl.ds(pl.multiple_of(rid * chunk, 8), chunk), :]
        for d in range(1, rcount):
            total = total + recv[rnd, d - 1]
        full[rnd, pl.ds(pl.multiple_of(rid * chunk, 8), chunk), :] = total
        for d in range(1, rcount):
            target = (rid + d) % rcount
            remote(
                own_rows(full, rnd, rid), own_rows(full, rnd, rid), ag_sem.at[0, rnd], ag_sem.at[1, rnd],
                grid.reduce_peer(target),
            ).start()
        others = full.at[rnd, pl.ds(0, ROWS - chunk)]
        ag_done = remote(others, others, ag_sem.at[0, rnd], ag_sem.at[1, rnd], grid.reduce_peer(rid))
        ag_done.wait_recv()

        head = full[rnd, 0:64, :]

        def scalars(j):
            return jnp.concatenate([head[14:15, j : j + 1], head[46:47, j : j + 1]], axis=0)

        norm, res_hard, cross, res_total = [scalars(j) for j in range(4)]
        if rnd == 0:
            dir_hard, dir_total = res_hard, res_total
            beta = jnp.zeros_like(norm)
        else:
            beta = norm / norm_old
            dir_hard = res_hard + 2.0 * beta * cross + beta * beta * dir_hard
            dir_total = res_total + beta * dir_total
        beta_rows = jnp.where(row64 < 32, beta[0:1], beta[1:2])
        s_all = []
        for i in range(6):
            s = full[rnd, pl.ds(i * 64, 64), :]
            if rnd > 0:
                s = s + beta_rows * s_dir[i]
            s_dir[i] = s
            s_all.append(s)
        q_cos, q_sin = [], []
        for i in range(3):
            both, diff = w_sum[i], w_dif[i]
            for k, out in ((0, q_cos), (1, q_sin)):
                mine, other = s_all[3 * k + i], s_all[3 * (1 - k) + i]
                sign = -1.0 if k == 0 else 1.0
                parts = []
                for rhs in (0, 32):
                    for t in (0, 1):
                        same = mine[rhs + 16 * t : rhs + 16 * t + 16]
                        swap = other[rhs + 16 * (1 - t) : rhs + 16 * (1 - t) + 16]
                        sign = -1.0 if t == k else 1.0
                        parts.append(both * same + sign * (diff * swap))
                out.append(jnp.concatenate(parts, axis=0))
        q_all = q_cos + q_sin
        energy = functools.reduce(jnp.add, [q * s for q, s in zip(q_all, s_all)])
        energy = lane_sum(energy)
        energy = jnp.concatenate(
            [jnp.sum(energy[0:32], axis=0, keepdims=True), jnp.sum(energy[32:64], axis=0, keepdims=True)], axis=0
        )
        alpha = norm / (dir_hard + energy)
        p = r + beta * p
        sol[...] += alpha * p
        step_total = alpha * dir_total
        sol_total = step_total if rnd == 0 else sol_total + step_total
        norm_old = norm
        if rnd + 1 < ITERS:
            direc[...] = p
            q_full = jnp.concatenate(q_all, axis=1)
            top = q_full.astype(BF16)
            qq = jnp.concatenate([top, (q_full - top.astype(F32)).astype(BF16)], axis=0)
            piece = 512 if atoms % 512 == 0 else atoms
            for j in range(atoms // piece):
                lanes = pl.ds(j * piece, piece)
                g = dot(qq, table[:, lanes])
                g = g[0:64] + g[64:128]
                xf = xfac[:, lanes]
                pot = jnp.concatenate(
                    [jnp.sum(g[k * 32 : k * 32 + 32] * xf, axis=0, keepdims=True) for k in range(2)], axis=0
                )
                applied = hard_all[:, lanes] * direc[:, lanes] + pot
                res[:, lanes] = res[:, lanes] - alpha * applied

    ratio = sol_total[0:1] / sol_total[1:2]
    mine = sol[:, pl.ds(pl.multiple_of(gid * A, A), A)]
    charge_ref[...] = mine[0:1] - ratio * mine[1:2]

    pos_done.wait_send()
    en_done.wait_send()
    for rnd in range(ITERS):
        remote(recv.at[rnd], recv.at[rnd], rs_sem.at[0, rnd], rs_sem.at[1, rnd], grid.reduce_peer(rid)).wait_send()
        others = full.at[rnd, pl.ds(0, ROWS - chunk)]
        remote(others, others, ag_sem.at[0, rnd], ag_sem.at[1, rnd], grid.reduce_peer(rid)).wait_send()


def split_sizes(mesh):
    dom, kv = mesh.shape["dom"], mesh.shape["kv"]
    shapes = {64: (4, 8, 2), 8: (2, 2, 2)}
    ny, nz, nc = shapes[dom]
    return ny, nz, nc, kv


def solution(mesh):
    sizes = split_sizes(mesh)
    ny, nz, nc, nx = sizes
    gcount, rcount = nz * nc, nx * ny
    atoms = gcount * A
    chunk = ROWS // rcount

    def local(
        node_feats, positions, species, halo_rows, neighbours, nbr_count, recip_vectors,
        w_msg, w_rad1, w_rad2, w_upd, w_out, chi_table, hard_table,
    ):
        vmem = pl.BlockSpec(memory_space=pltpu.VMEM)
        smem = pl.BlockSpec(memory_space=pltpu.SMEM)
        electroneg, charges = pl.pallas_call(
            functools.partial(kernel, sizes),
            out_shape=(jax.ShapeDtypeStruct((1, A), F32), jax.ShapeDtypeStruct((1, A), F32)),
            in_specs=[vmem] * 12 + [smem] * 2,
            out_specs=(vmem, vmem),
            scratch_shapes=[
                pltpu.VMEM((TROWS, A), BF16),
                pltpu.VMEM((TROWS, A), BF16),
                pltpu.VMEM((2, TROWS, A), BF16),
                pltpu.VMEM((gcount, 8, A), F32),
                pltpu.VMEM((gcount, 8, A), F32),
                pltpu.VMEM((TROWS, 2 * A), BF16),
                pltpu.VMEM((NBR, A), I32),
                pltpu.VMEM((4, A, A), F32),
                pltpu.VMEM((A, A), BF16),
                pltpu.VMEM((2 * A, A), BF16),
                pltpu.VMEM((A, 3 * A), BF16),
                pltpu.VMEM((2 * HALF, atoms), BF16),
                pltpu.VMEM((32, atoms), F32),
                pltpu.VMEM((1, atoms), F32),
                pltpu.VMEM((128, atoms), BF16),
                pltpu.VMEM((2, atoms), F32),
                pltpu.VMEM((2, atoms), F32),
                pltpu.VMEM((2, atoms), F32),
                pltpu.VMEM((ITERS, ROWS, A), F32),
                pltpu.VMEM((ITERS, rcount - 1, chunk, A), F32),
                pltpu.VMEM((ITERS, ROWS, A), F32),
                pltpu.VMEM((32, HALF), F32),
                pltpu.VMEM((3, 16, A), F32),
                pltpu.VMEM((3, 16, A), F32),
                pltpu.VMEM((6, 64, A), F32),
                pltpu.SemaphoreType.DMA((4,)),
                pltpu.SemaphoreType.DMA((2,)),
                pltpu.SemaphoreType.DMA((2,)),
                pltpu.SemaphoreType.DMA((2, ITERS)),
                pltpu.SemaphoreType.DMA((2, ITERS)),
            ],
            compiler_params=pltpu.CompilerParams(
                collective_id=0, has_side_effects=True, vmem_limit_bytes=48 * 1024 * 1024
            ),
        )(
            node_feats, positions, species.reshape(1, A), halo_rows, neighbours, nbr_count.reshape(1, A),
            recip_vectors, w_msg, w_rad1, w_rad2, w_upd, w_out.reshape(1, A), chi_table, hard_table,
        )
        return electroneg.reshape(A), charges.reshape(A)

    both = ("dom", "kv")
    return jax.shard_map(
        local,
        mesh=mesh,
        in_specs=(
            P(both, None), P(None, both), P(both), P(both, None), P(both, None), P(both),
            P(), P(), P(), P(), P(), P(), P(), P(),
        ),
        out_specs=(P(both), P(both)),
        check_vma=False,
    )
```

time: 1830 us -> 81.4 us (0.04)
  the two profiles are of different devices: /device:TPU:1 before, /device:TPU:8 now
where the time goes in v1:
time: 81.4 us; the launch traced here: 81 us
  Pallas kernels  74.9 us (92%)
  local copies, waits for them, and re-layouts  5.29 us (6%)
    pallas_call x1, Pallas kernels, local(): pl.pallas_call(functools.partial(kernel, sizes), out_shape=(jax.ShapeDtyp...  74.9 us
    unnamed x29, local copies, waits for them, and re-layouts  5.29 us

profile of v1, /device:TPU:8, one launch (start us, length us, event | category | flops | bytes accessed | tf_op | source)
XLA Modules:
  0.0 81.0 jit_solution(16005246747294974894)
XLA Ops:
  0.6 0.0 copy-start.2
  0.6 0.0 copy-start.5
  0.7 0.0 copy-start.6
  0.7 0.0 copy-start.7
  0.7 0.0 copy-start.8
  0.7 0.0 copy-start.9
  0.7 0.0 copy-start.10
  0.7 0.0 copy-start.11
  0.7 0.0 copy-start.12
  0.7 0.9 %copy.16.nbr_ref = s32[128,32]{1,0:T(8,128)S(1)} copy(s32[128,32]{0,1:T(8,128)} %param.18) | data formatting | bytes 32768 | tf_op args[4]
  1.6 0.0 copy-done.2
  1.6 0.0 copy-done.5
  1.6 0.0 copy-done.6
  1.6 0.0 copy-done.7
  1.6 0.0 copy-done.8
  1.7 0.0 copy-done.9
  1.7 0.0 copy-done.10
  1.7 0.0 copy-done.11
  1.7 0.0 copy-done.12
  1.7 0.0 copy-start
  1.7 0.9 %copy-done = s32[3,16384]{1,0:T(4,128)S(1)} copy-done((s32[3,16384]{1,0:T(4,128)S(1)}, s32[3,16384]{1,0:T(4,128)}, u32[]{:S(2)}) %copy-start) | copy-done | bytes 196632
  2.6 0.0 copy-start.1
  2.6 0.9 %copy-done.1 = bf16[384,128]{1,0:T(8,128)(2,1)S(1)} copy-done((bf16[384,128]{1,0:T(8,128)(2,1)S(1)}, bf16[384,128]{1,0:T(8,128)(2,1)}, u32[]{:S(2)}) %copy-start.1) | copy-done | bytes 98328
  3.5 0.0 copy-start.3
  3.5 0.8 copy-done.3
  4.3 0.0 copy-start.4
  4.3 0.8 copy-done.4
  5.1 74.9 %shard_map.149 = (f32[1,128]{1,0:T(1,128)S(1)}, f32[1,128]{1,0:T(1,128)S(1)}) custom-call(bf16[128,128]{1,0:T(8,128)(2,1)S(1)} %copy-done.3, f32[3,128]{1,0:T(4,128)S(1)} %copy-done.5, s32[1,128]{1,0:T(1,128)S(1)} %bitcast.5, s32[1,64]{1,0:T(1,128)S(1)} %copy-done.8, s32[128,32]{1,0:T(8,128)S(1)} %copy.16.nbr_ref, s32[1,128]{1,0:T(1,128)S(1)} %bitcast.6, ...), custom_call_target="tpu_custom_call" | custom-call | tf_op jit(solution)/shard_map/pallas_call | solution.py:481
  80.0 0.5 copy.19
  80.5 0.5 copy.20
Async XLA Ops:
  0.6 1.0 %copy-start.2 = (bf16[128,256]{1,0:T(8,128)(2,1)S(1)}, bf16[128,256]{1,0:T(8,128)(2,1)}, u32[]{:S(2)}) copy-start(bf16[128,256]{1,0:T(8,128)(2,1)} %w_rad2_ref.1) | copy-start | bytes 196612
  0.6 1.0 %copy-start.5 = (f32[3,128]{1,0:T(4,128)S(1)}, f32[3,128]{1,0:T(4,128)}, u32[]{:S(2)}) copy-start(f32[3,128]{1,0:T(4,128)} %pos_ref.1) | copy-start | bytes 4612
  0.7 1.0 %copy-start.6 = (bf16[8,128]{1,0:T(8,128)(2,1)S(1)}, bf16[8,128]{1,0:T(8,128)(2,1)}, u32[]{:S(2)}) copy-start(bf16[8,128]{1,0:T(8,128)(2,1)} %w_rad1_ref.1) | copy-start | bytes 6148
  0.7 1.0 %copy-start.7 = (s32[128]{0:T(128)S(1)}, s32[128]{0:T(128)}, u32[]{:S(2)}) copy-start(s32[128]{0:T(128)} %param.16) | copy-start | bytes 1540
  0.7 1.0 %copy-start.8 = (s32[1,64]{1,0:T(1,128)S(1)}, s32[1,64]{1,0:T(1,128)}, u32[]{:S(2)}) copy-start(s32[1,64]{1,0:T(1,128)} %halo_ref.1) | copy-start | bytes 772
  0.7 1.0 %copy-start.9 = (s32[128]{0:T(128)S(1)}, s32[128]{0:T(128)}, u32[]{:S(2)}) copy-start(s32[128]{0:T(128)} %param.19) | copy-start | bytes 1540
  0.7 1.0 %copy-start.10 = (bf16[128]{0:T(256)(128)(2,1)S(1)}, bf16[128]{0:T(256)(128)(2,1)}, u32[]{:S(2)}) copy-start(bf16[128]{0:T(256)(128)(2,1)} %param.25) | copy-start | bytes 772
  0.7 1.0 %copy-start.11 = (f32[2]{0:T(128)S(1)}, f32[2]{0:T(128)}, u32[]{:S(2)}) copy-start(f32[2]{0:T(128)} %chi_ref.1) | copy-start | bytes 28
  0.7 1.0 %copy-start.12 = (f32[2]{0:T(128)S(1)}, f32[2]{0:T(128)}, u32[]{:S(2)}) copy-start(f32[2]{0:T(128)} %hard_ref.1) | copy-start | bytes 28
  1.7 1.0 %copy-start = (s32[3,16384]{1,0:T(4,128)S(1)}, s32[3,16384]{1,0:T(4,128)}, u32[]{:S(2)}) copy-start(s32[3,16384]{1,0:T(4,128)} %recip_ref.1) | copy-start | bytes 589828
  2.6 0.9 %copy-start.1 = (bf16[384,128]{1,0:T(8,128)(2,1)S(1)}, bf16[384,128]{1,0:T(8,128)(2,1)}, u32[]{:S(2)}) copy-start(bf16[384,128]{1,0:T(8,128)(2,1)} %w_upd_ref.1) | copy-start | bytes 294916
  3.5 0.8 copy-start.3
  4.3 0.8 copy-start.4

commit v2 on v1

--- a/solution.py
+++ b/solution.py
@@ -16,7 +16,7 @@
 A = 128
 NBR = 32
 HALF = 384
-ROWS = 6 * 64
+CHUNKS = 24
 TROWS = 160
 TURN = 2.0 * math.pi
 SIN_C = [(-1.0) ** k * TURN ** (2 * k + 1) / math.factorial(2 * k + 1) for k in range(10)]
@@ -55,6 +55,10 @@
     return lax.broadcasted_iota(I32, shape, dim)
 
 
+def ring(step, count):
+    return min(step, count - step)
+
+
 class Grid:
     def __init__(self, sizes):
         self.sizes = sizes
@@ -62,18 +66,23 @@
         dom, x = lax.axis_index("dom"), lax.axis_index("kv")
         self.y, self.z, self.c, self.x = dom // (nz * nc), (dom // nc) % nz, dom % nc, x
         self.dom = dom
-        self.reduce_count = nx * ny
-        self.gather_count = nz * nc
-        self.reduce_id = self.y * nx + self.x
-        self.gather_id = self.z * nc + self.c
-
-    def reduce_peer(self, index):
+        steps = [(dx, dy, dc) for dx in range(nx) for dy in range(ny) for dc in range(nc)]
+        steps.sort(key=lambda s: (-(ring(s[0], nx) + ring(s[1], ny)), s))
+        self.peers = []
+        for dx, dy, dc in steps:
+            if dx or dy or dc:
+                px, py, pc = (x + dx) % nx, (self.y + dy) % ny, (self.c + dc) % nc
+                self.peers.append(({"dom": (py * nz + self.z) * nc + pc, "kv": px}, *self.share(px, py, pc)))
+        self.chunk, self.owner = self.share(x, self.y, self.c)
+        self.column = []
+        for dz in sorted(range(1, nz), key=lambda d: -ring(d, nz)):
+            self.column.append({"dom": (self.y * nz + (self.z + dz) % nz) * nc + self.c, "kv": x})
+
+    def share(self, x, y, c):
         ny, nz, nc, nx = self.sizes
-        return {"dom": ((index // nx) * nz + self.z) * nc + self.c, "kv": index % nx}
-
-    def gather_peer(self, index):
-        ny, nz, nc, nx = self.sizes
-        return {"dom": self.y * (nz * nc) + index, "kv": self.x}
+        index = (y * nx + x) * nc + c
+        part = index % 4
+        return (index // 4) * 3 + jnp.minimum(part, 2), part < 3
 
     def slab_peer(self, step):
         ny, nz, nc, nx = self.sizes
@@ -84,88 +93,77 @@
 
 def kernel(
     sizes,
-    feats_ref,
-    pos_ref,
-    species_ref,
-    halo_ref,
-    nbr_ref,
-    count_ref,
-    recip_ref,
-    w_msg_ref,
-    w_rad1_ref,
-    w_rad2_ref,
-    w_upd_ref,
-    w_out_ref,
-    chi_ref,
-    hard_ref,
-    en_ref,
-    charge_ref,
-    own_tab,
-    packet,
-    got,
-    pos_all,
-    en_all,
-    nbr_tab,
-    slots,
-    acc,
-    w_rad1_t,
-    w_rad2_t,
-    w_upd_t,
-    table,
-    xfac,
-    hard_all,
-    ff,
-    res,
-    direc,
-    sol,
-    pay,
-    recv,
-    full,
-    present,
-    w_sum,
-    w_dif,
-    s_dir,
-    halo_sem,
-    pos_sem,
-    en_sem,
-    rs_sem,
-    ag_sem,
+    *refs,
 ):
+    inputs, out_ref, arrived, scratch = refs[:14], refs[14], refs[15:29], refs[29:]
+    (
+        own_tab,
+        packet,
+        got,
+        pos_all,
+        en_all,
+        nbr_tab,
+        slots,
+        acc,
+        w_rad1_t,
+        w_rad2_t,
+        w_upd_t,
+        table,
+        xfac,
+        hard_all,
+        ff,
+        res,
+        direc,
+        sol,
+        pay,
+        recv,
+        full,
+        present,
+        w_sum,
+        w_dif,
+        s_dir,
+        halo_sem,
+        pos_sem,
+        en_sem,
+        rs_sem,
+        ag_sem,
+        in_sem,
+    ) = scratch
+    (
+        feats_ref, pos_ref, species_ref, halo_ref, nbr_ref, count_ref, recip_ref, w_msg_ref, w_rad1_ref, w_rad2_ref,
+        w_upd_ref, w_out_ref, chi_ref, hard_ref,
+    ) = arrived
     grid = Grid(sizes)
-    gcount, rcount = grid.gather_count, grid.reduce_count
-    gid, rid = grid.gather_id, grid.reduce_id
-    atoms = gcount * A
-    atoms_total = atoms * rcount
+    nz = sizes[1]
+    gid = grid.z
+    atoms = nz * A
+    peers, column = grid.peers, grid.column
+    atoms_total = atoms * (len(peers) + 1)
     box_x = (atoms_total // A) * SLAB_W
-    chunk = ROWS // rcount
     kvec = recip_ref.shape[1]
 
+    loads = [pltpu.make_async_copy(src, dst, in_sem.at[i]) for i, (src, dst) in enumerate(zip(inputs, arrived))]
+    for i in (0, 7, 1, 3, 2, 13, 4, 5, 6, 8, 9, 10, 11, 12):
+        loads[i].start()
+
     barrier = pltpu.get_barrier_semaphore()
-
-    def greet(device):
+    partners = [grid.slab_peer(-1), grid.slab_peer(1)] + column + [device for device, _, _ in peers]
+    for device in partners:
         pl.semaphore_signal(barrier, inc=1, device_id=device, device_id_type=MESH)
-
-    greet(grid.slab_peer(-1))
-    greet(grid.slab_peer(1))
-    for d in range(1, gcount):
-        greet(grid.gather_peer((gid + d) % gcount))
-    for d in range(1, rcount):
-        greet(grid.reduce_peer((rid + d) % rcount))
 
     def remote(src, dst, send, recv_, device):
         return pltpu.make_async_remote_copy(
             src_ref=src, dst_ref=dst, send_sem=send, recv_sem=recv_, device_id=device, device_id_type=MESH
         )
 
-    def own_rows(ref, rnd, index):
-        return ref.at[rnd, pl.ds(pl.multiple_of(index * chunk, 8), chunk)]
-
+    for i in (0, 1, 2, 3, 7, 13):
+        loads[i].wait()
     species = species_ref[...]
-    hardness = jnp.where(species == 0, hard_ref[0], hard_ref[1])
+    hard = hard_ref[...]
+    hardness = jnp.where(species == 0, hard[0:1, 0:1], hard[0:1, 1:2])
     pos = jnp.concatenate([pos_ref[...], jnp.zeros((5, A), F32)], axis=0)
     pos_all[gid] = jnp.concatenate([pos_ref[...], hardness, jnp.zeros((4, A), F32)], axis=0)
-    feats_t = transposed(feats_ref[...])
-    proj_t = dot(transposed(w_msg_ref[...]).astype(BF16), feats_t.astype(BF16))
+    proj_t = dot(feats_ref[...], w_msg_ref[...]).T
     hi = pos.astype(BF16).astype(F32)
     mid = (pos - hi).astype(BF16).astype(F32)
     low = pos - hi - mid
@@ -173,6 +171,30 @@
     halo = jnp.concatenate([halo_ref[...], halo_ref[...]], axis=1)
     pick = jnp.where(iota((A, A), 0) == halo, 1.0, 0.0).astype(BF16)
     packet[...] = dot(own_tab[...], pick).astype(BF16)
+
+    pl.semaphore_wait(barrier, len(partners))
+
+    to_left = remote(packet, got.at[1], halo_sem.at[0], halo_sem.at[3], grid.slab_peer(-1))
+    to_right = remote(packet, got.at[0], halo_sem.at[1], halo_sem.at[2], grid.slab_peer(1))
+    to_left.start()
+    to_right.start()
+    for device in column:
+        remote(pos_all.at[gid], pos_all.at[gid], pos_sem.at[0], pos_sem.at[1], device).start()
+
+    for i in (4, 5, 6, 8, 9, 10, 11, 12):
+        loads[i].wait()
+    w_rad1_t[...] = jnp.concatenate(
+        [transposed(jnp.concatenate([w_rad1_ref[...].astype(F32), jnp.zeros((120, A), F32)], axis=0))], axis=1
+    ).astype(BF16)
+    for i in range(2):
+        w_rad2_t[pl.ds(i * A, A), :] = transposed(w_rad2_ref[:, i * A : (i + 1) * A]).astype(BF16)
+    for i in range(3):
+        w_upd_t[:, pl.ds(i * A, A)] = transposed(w_upd_ref[i * A : (i + 1) * A, :]).astype(BF16)
+    index = nbr_ref[...]
+    place = jnp.where(index < A, index, jnp.where(index < A + 32, index + 32, index - 32))
+    slots[...] = jnp.where(iota((NBR, A), 0) < count_ref[...], place, -1)
+    nbr_tab[:, 0:A] = own_tab[...]
+    feats_t = transposed(feats_ref[...])
 
     k_step = 2048 if kvec % 2048 == 0 else kvec
     present[...] = jnp.zeros((32, HALF), F32)
@@ -190,43 +212,8 @@
         return carry
 
     k_steps = kvec // k_step
-    lax.fori_loop(0, k_steps // 2, count_triples, 0)
-
-    pl.semaphore_wait(barrier, 2 + gcount - 1 + rcount - 1)
-
-    to_left = remote(packet, got.at[1], halo_sem.at[0], halo_sem.at[3], grid.slab_peer(-1))
-    to_right = remote(packet, got.at[0], halo_sem.at[1], halo_sem.at[2], grid.slab_peer(1))
-    to_left.start()
-    to_right.start()
-    for d in range(1, gcount):
-        peer = grid.gather_peer((gid + d) % gcount)
-        remote(pos_all.at[gid], pos_all.at[gid], pos_sem.at[0], pos_sem.at[1], peer).start()
-
-    lax.fori_loop(k_steps // 2, k_steps, count_triples, 0)
-    column = iota((1, HALF), 1)
-    late = column - 336
-    grid_y = jnp.where(late < 0, (column * 2731) >> 16, late & 15)
-    grid_z = jnp.where(late < 0, column - grid_y * 24 - 13, 11 + (late >> 4))
-    grid_x = iota((16, 1), 0)
-    m_square = (grid_y * grid_y + grid_z * grid_z + grid_x * grid_x).astype(F32)
-    weight = 16.0 / atoms_total * jnp.exp(-m_square / 400.0) / (1.0 + m_square / 16.0)
-    plus, minus = present[0:16] * weight, present[16:32] * weight
-    for i in range(3):
-        lanes = slice(i * 128, (i + 1) * 128)
-        w_sum[i] = (plus + minus)[:, lanes]
-        w_dif[i] = (plus - minus)[:, lanes]
-
-    w_rad1_t[...] = jnp.concatenate(
-        [transposed(jnp.concatenate([w_rad1_ref[...].astype(F32), jnp.zeros((120, A), F32)], axis=0))], axis=1
-    ).astype(BF16)
-    for i in range(2):
-        w_rad2_t[pl.ds(i * A, A), :] = transposed(w_rad2_ref[:, i * A : (i + 1) * A]).astype(BF16)
-    for i in range(3):
-        w_upd_t[:, pl.ds(i * A, A)] = transposed(w_upd_ref[i * A : (i + 1) * A, :]).astype(BF16)
-    index = jnp.concatenate([nbr_ref[...].astype(F32), jnp.zeros((A, A - NBR), F32)], axis=1).T[0:NBR].astype(I32)
-    place = jnp.where(index < A, index, jnp.where(index < A + 32, index + 32, index - 32))
-    slots[...] = jnp.where(iota((NBR, A), 0) < count_ref[...], place, -1)
-    nbr_tab[:, 0:A] = own_tab[...]
+    H1, H2 = k_steps // 4, 3 * k_steps // 4
+    lax.fori_loop(0, H1, count_triples, 0)
 
     to_left.wait_send()
     to_right.wait_send()
@@ -280,15 +267,15 @@
     joined = jnp.concatenate([acc[0] * scale, vec_square, feats_t], axis=0).astype(BF16)
     update = silu(dot(w_upd_t[...], joined)).astype(BF16)
     w_out = jnp.broadcast_to(w_out_ref[...].astype(F32), (16, A)).astype(BF16)
-    electroneg = dot(w_out, update)[0:1] + jnp.where(species == 0, chi_ref[0], chi_ref[1])
-    en_ref[...] = electroneg
+    chi = chi_ref[...]
+    electroneg = dot(w_out, update)[0:1] + jnp.where(species == 0, chi[0:1, 0:1], chi[0:1, 1:2])
+    out_ref[0:1, :] = electroneg
     en_all[gid] = jnp.broadcast_to(electroneg, (8, A))
-    for d in range(1, gcount):
-        peer = grid.gather_peer((gid + d) % gcount)
-        remote(en_all.at[gid], en_all.at[gid], en_sem.at[0], en_sem.at[1], peer).start()
+    for device in column:
+        remote(en_all.at[gid], en_all.at[gid], en_sem.at[0], en_sem.at[1], device).start()
 
     def gathered(ref, sem):
-        return remote(ref.at[pl.ds(0, gcount - 1)], ref.at[pl.ds(0, gcount - 1)], sem.at[0], sem.at[1], grid.gather_peer(gid))
+        return remote(ref.at[pl.ds(0, nz - 1)], ref.at[pl.ds(0, nz - 1)], sem.at[0], sem.at[1], column[0])
 
     pos_done = gathered(pos_all, pos_sem)
     pos_done.wait_recv()
@@ -316,7 +303,8 @@
         table[HALF : 2 * HALF, lanes] = jnp.concatenate(sin_rows, axis=0).astype(BF16)
         return carry
 
-    lax.fori_loop(0, gcount, build, 0)
+    lax.fori_loop(0, nz, build, 0)
+    lax.fori_loop(H1, H2, count_triples, 0)
 
     en_done = gathered(en_all, en_sem)
     en_done.wait_recv()
@@ -327,7 +315,7 @@
         res[:, lanes] = jnp.where(iota((2, A), 0) == 0, -tile[0:2], 1.0)
         return carry
 
-    lax.fori_loop(0, gcount, start_residual, 0)
+    lax.fori_loop(0, nz, start_residual, 0)
     sol[...] = jnp.zeros(sol.shape, F32)
     direc[...] = jnp.zeros(direc.shape, F32)
     s_dir[...] = jnp.zeros(s_dir.shape, F32)
@@ -337,6 +325,9 @@
 
     def lane_sum(v):
         return jnp.sum(v, axis=1, keepdims=True)
+
+    def all_in(ref, sem, rnd):
+        return remote(ref, ref, sem.at[0, rnd], sem.at[1, rnd], column[0])
 
     norm_old = dir_hard = dir_total = sol_total = None
     for rnd in range(ITERS):
@@ -350,42 +341,62 @@
         extra = jnp.zeros((64, A), F32)
         for k in range(2):
             for j in range(4):
-                extra = jnp.where((row64 == k * 32 + 14) & (lane64 == j), sums[j][k : k + 1], extra)
+                top = sums[j][k : k + 1].astype(BF16).astype(F32)
+                extra = jnp.where((row64 == k * 32 + 14) & (lane64 == j), top, extra)
+                extra = jnp.where((row64 == k * 32 + 15) & (lane64 == j), sums[j][k : k + 1] - top, extra)
         for j in range(3):
             s = dot_nt(ff[...], table[pl.ds(j * 256, 256), :])
             s = s[0:64] + s[64:128]
             left = s[:, 0:128]
             if j == 0:
                 left = left + extra
-            pay[rnd, pl.ds(j * 128, 64), :] = left
-            pay[rnd, pl.ds(j * 128 + 64, 64), :] = s[:, 128:256]
-
-        for d in range(1, rcount):
-            target = (rid + d) % rcount
-            remote(
-                own_rows(pay, rnd, target), recv.at[rnd, d - 1], rs_sem.at[0, rnd], rs_sem.at[1, rnd],
-                grid.reduce_peer(target),
-            ).start()
-        rs_done = remote(recv.at[rnd], recv.at[rnd], rs_sem.at[0, rnd], rs_sem.at[1, rnd], grid.reduce_peer(rid))
-        rs_done.wait_recv()
-        total = pay[rnd, pl.ds(pl.multiple_of(rid * chunk, 8), chunk), :]
-        for d in range(1, rcount):
-            total = total + recv[rnd, d - 1]
-        full[rnd, pl.ds(pl.multiple_of(rid * chunk, 8), chunk), :] = total
-        for d in range(1, rcount):
-            target = (rid + d) % rcount
-            remote(
-                own_rows(full, rnd, rid), own_rows(full, rnd, rid), ag_sem.at[0, rnd], ag_sem.at[1, rnd],
-                grid.reduce_peer(target),
-            ).start()
-        others = full.at[rnd, pl.ds(0, ROWS - chunk)]
-        ag_done = remote(others, others, ag_sem.at[0, rnd], ag_sem.at[1, rnd], grid.reduce_peer(rid))
-        ag_done.wait_recv()
-
-        head = full[rnd, 0:64, :]
+            pay[rnd, pl.ds(8 * j, 4)] = left.astype(BF16).reshape(4, 16, A)
+            pay[rnd, pl.ds(8 * j + 4, 4)] = s[:, 128:256].astype(BF16).reshape(4, 16, A)
+
+        for k, (device, share, owns) in enumerate(peers):
+
+            @pl.when(owns)
+            def _():
+                remote(pay.at[rnd, share], recv.at[rnd, k], rs_sem.at[0, rnd], rs_sem.at[1, rnd], device).start()
+
+        if rnd == 0:
+            lax.fori_loop(H2, k_steps, count_triples, 0)
+            column_id = iota((1, HALF), 1)
+            late = column_id - 336
+            grid_y = jnp.where(late < 0, (column_id * 2731) >> 16, late & 15)
+            grid_z = jnp.where(late < 0, column_id - grid_y * 24 - 13, 11 + (late >> 4))
+            grid_x = iota((16, 1), 0)
+            m_square = (grid_y * grid_y + grid_z * grid_z + grid_x * grid_x).astype(F32)
+            weight = 16.0 / atoms_total * jnp.exp(-m_square / 400.0) / (1.0 + m_square / 16.0)
+            plus, minus = present[0:16] * weight, present[16:32] * weight
+            for i in range(3):
+                lanes = slice(i * 128, (i + 1) * 128)
+                w_sum[i] = (plus + minus)[:, lanes]
+                w_dif[i] = (plus - minus)[:, lanes]
+
+        @pl.when(grid.owner)
+        def _():
+            all_in(recv.at[rnd], rs_sem, rnd).wait_recv()
+            total = pay[rnd, grid.chunk].astype(F32)
+            for k in range(len(peers)):
+                total = total + recv[rnd, k].astype(F32)
+            scalar = total[14:15] + total[15:16]
+            top = scalar.astype(BF16).astype(F32)
+            full[rnd, grid.chunk] = jnp.concatenate([total[0:14], top, scalar - top], axis=0).astype(BF16)
+            for device, _, _ in peers:
+                mine = full.at[rnd, grid.chunk]
+                remote(mine, mine, ag_sem.at[0, rnd], ag_sem.at[1, rnd], device).start()
+            all_in(full.at[rnd, pl.ds(0, CHUNKS - 1)], ag_sem, rnd).wait_recv()
+
+        @pl.when(jnp.logical_not(grid.owner))
+        def _():
+            all_in(full.at[rnd], ag_sem, rnd).wait_recv()
+
+        head = full[rnd, 0:4].reshape(64, A).astype(F32)
 
         def scalars(j):
-            return jnp.concatenate([head[14:15, j : j + 1], head[46:47, j : j + 1]], axis=0)
+            both = [head[k + 14 : k + 15, j : j + 1] + head[k + 15 : k + 16, j : j + 1] for k in (0, 32)]
+            return jnp.concatenate(both, axis=0)
 
         norm, res_hard, cross, res_total = [scalars(j) for j in range(4)]
         if rnd == 0:
@@ -398,7 +409,7 @@
         beta_rows = jnp.where(row64 < 32, beta[0:1], beta[1:2])
         s_all = []
         for i in range(6):
-            s = full[rnd, pl.ds(i * 64, 64), :]
+            s = full[rnd, pl.ds(i * 4, 4)].reshape(64, A).astype(F32)
             if rnd > 0:
                 s = s + beta_rows * s_dir[i]
             s_dir[i] = s
@@ -448,47 +459,50 @@
 
     ratio = sol_total[0:1] / sol_total[1:2]
     mine = sol[:, pl.ds(pl.multiple_of(gid * A, A), A)]
-    charge_ref[...] = mine[0:1] - ratio * mine[1:2]
+    out_ref[1:2, :] = mine[0:1] - ratio * mine[1:2]
 
     pos_done.wait_send()
     en_done.wait_send()
     for rnd in range(ITERS):
-        remote(recv.at[rnd], recv.at[rnd], rs_sem.at[0, rnd], rs_sem.at[1, rnd], grid.reduce_peer(rid)).wait_send()
-        others = full.at[rnd, pl.ds(0, ROWS - chunk)]
-        remote(others, others, ag_sem.at[0, rnd], ag_sem.at[1, rnd], grid.reduce_peer(rid)).wait_send()
-
-
-def split_sizes(mesh):
-    dom, kv = mesh.shape["dom"], mesh.shape["kv"]
-    shapes = {64: (4, 8, 2), 8: (2, 2, 2)}
-    ny, nz, nc = shapes[dom]
-    return ny, nz, nc, kv
+
+        @pl.when(grid.owner)
+        def _():
+            all_in(pay.at[rnd, pl.ds(0, CHUNKS - 1)], rs_sem, rnd).wait_send()
+            all_in(recv.at[rnd], ag_sem, rnd).wait_send()
+
+        @pl.when(jnp.logical_not(grid.owner))
+        def _():
+            all_in(pay.at[rnd], rs_sem, rnd).wait_send()
 
 
 def solution(mesh):
-    sizes = split_sizes(mesh)
+    sizes = (4, 8, 2, 4)
     ny, nz, nc, nx = sizes
-    gcount, rcount = nz * nc, nx * ny
-    atoms = gcount * A
-    chunk = ROWS // rcount
+    assert dict(mesh.shape) == {"dom": ny * nz * nc, "kv": nx}
+    atoms = nz * A
+    others = nx * ny * nc - 1
 
     def local(
         node_feats, positions, species, halo_rows, neighbours, nbr_count, recip_vectors,
         w_msg, w_rad1, w_rad2, w_upd, w_out, chi_table, hard_table,
     ):
-        vmem = pl.BlockSpec(memory_space=pltpu.VMEM)
-        smem = pl.BlockSpec(memory_space=pltpu.SMEM)
-        electroneg, charges = pl.pallas_call(
+        operands = (
+            node_feats, positions, species.reshape(1, A), halo_rows, neighbours.T, nbr_count.reshape(1, A),
+            recip_vectors, w_msg, w_rad1, w_rad2, w_upd, w_out.reshape(1, A), chi_table.reshape(1, 2),
+            hard_table.reshape(1, 2),
+        )
+        out = pl.pallas_call(
             functools.partial(kernel, sizes),
-            out_shape=(jax.ShapeDtypeStruct((1, A), F32), jax.ShapeDtypeStruct((1, A), F32)),
-            in_specs=[vmem] * 12 + [smem] * 2,
-            out_specs=(vmem, vmem),
-            scratch_shapes=[
+            out_shape=jax.ShapeDtypeStruct((2, A), F32),
+            in_specs=[pl.BlockSpec(memory_space=pltpu.HBM)] * len(operands),
+            out_specs=pl.BlockSpec(memory_space=pltpu.VMEM),
+            scratch_shapes=[pltpu.VMEM(v.shape, v.dtype) for v in operands]
+            + [
                 pltpu.VMEM((TROWS, A), BF16),
                 pltpu.VMEM((TROWS, A), BF16),
                 pltpu.VMEM((2, TROWS, A), BF16),
-                pltpu.VMEM((gcount, 8, A), F32),
-                pltpu.VMEM((gcount, 8, A), F32),
+                pltpu.VMEM((nz, 8, A), F32),
+                pltpu.VMEM((nz, 8, A), F32),
                 pltpu.VMEM((TROWS, 2 * A), BF16),
                 pltpu.VMEM((NBR, A), I32),
                 pltpu.VMEM((4, A, A), F32),
@@ -502,9 +516,9 @@
                 pltpu.VMEM((2, atoms), F32),
                 pltpu.VMEM((2, atoms), F32),
                 pltpu.VMEM((2, atoms), F32),
-                pltpu.VMEM((ITERS, ROWS, A), F32),
-                pltpu.VMEM((ITERS, rcount - 1, chunk, A), F32),
-                pltpu.VMEM((ITERS, ROWS, A), F32),
+                pltpu.VMEM((ITERS, CHUNKS, 16, A), BF16),
+                pltpu.VMEM((ITERS, others, 16, A), BF16),
+                pltpu.VMEM((ITERS, CHUNKS, 16, A), BF16),
                 pltpu.VMEM((32, HALF), F32),
                 pltpu.VMEM((3, 16, A), F32),
                 pltpu.VMEM((3, 16, A), F32),
@@ -514,15 +528,13 @@
                 pltpu.SemaphoreType.DMA((2,)),
                 pltpu.SemaphoreType.DMA((2, ITERS)),
                 pltpu.SemaphoreType.DMA((2, ITERS)),
+                pltpu.SemaphoreType.DMA((len(operands),)),
             ],
             compiler_params=pltpu.CompilerParams(
-                collective_id=0, has_side_effects=True, vmem_limit_bytes=48 * 1024 * 1024
+                collective_id=0, has_side_effects=True, vmem_limit_bytes=60 * 1024 * 1024
             ),
-        )(
-            node_feats, positions, species.reshape(1, A), halo_rows, neighbours, nbr_count.reshape(1, A),
-            recip_vectors, w_msg, w_rad1, w_rad2, w_upd, w_out.reshape(1, A), chi_table, hard_table,
-        )
-        return electroneg.reshape(A), charges.reshape(A)
+        )(*operands)
+        return out[0], out[1]
 
     both = ("dom", "kv")
     return jax.shard_map(

time: 81.4 us -> 69.5 us (0.85)
  the two profiles are of different devices: /device:TPU:8 before, /device:TPU:1 now
where the time goes in v2:
time: 69.5 us; the launch traced here: 69.4 us
  Pallas kernels  67.5 us (97%)
  local copies, waits for them, and re-layouts  1.25 us (2%)
    pallas_call x1, Pallas kernels, local(): pl.pallas_call(functools.partial(kernel, sizes), out_shape=jax.ShapeDtype...  67.5 us

profile of v2, /device:TPU:1, one launch (start us, length us, event | category | flops | bytes accessed | tf_op | source)
XLA Modules:
  0.0 69.4 jit_solution(17393038138637128529)
XLA Ops:
  0.6 67.5 %shard_map.149 = f32[2,128]{1,0:T(2,128)} custom-call(bf16[128,128]{1,0:T(8,128)(2,1)} %refs_0_.1, f32[3,128]{1,0:T(4,128)} %refs_1_.1, s32[1,128]{1,0:T(1,128)} %bitcast.11, s32[1,64]{1,0:T(1,128)} %refs_3_.1, s32[32,128]{1,0:T(8,128)} %bitcast.10, s32[1,128]{1,0:T(1,128)} %bitcast.12, s32[3,16384]{1,0:T(4,128)} %refs_6_.1, bf16[128,128]{1,0:T(8,128)(2,1)} %refs_7_.1, ...), custom_call_target="tpu_custom_call" | custom-call | tf_op jit(solution)/shard_map/pallas_call | solution.py:494
  68.2 1.3 %slice_bitcast_fusion = (f32[128]{0:T(128)}, f32[128]{0:T(128)}) fusion(f32[2,128]{1,0:T(2,128)} %shard_map.149), kind=kLoop, calls=%fused_computation | loop fusion | bytes 2048 | tf_op jit(solution)/shard_map/squeeze | solution.py:537

commit v3 on v2

--- a/solution.py
+++ b/solution.py
@@ -49,6 +49,18 @@
 
 def transposed(v):
     return v.astype(F32).T
+
+
+def coded(v):
+    top = jnp.max(jnp.abs(v), axis=0, keepdims=True)
+    power = jnp.ceil(jnp.log2(jnp.maximum(top, 1e-30) * 1.01)) - 15.0
+    whole = jnp.round(v * jnp.exp2(-power))
+    return jnp.where(iota(v.shape, 0) == 15, power, whole).astype(I32).astype(jnp.int16)
+
+
+def decoded(q):
+    v = q.astype(I32).astype(F32)
+    return v * jnp.exp2(v[15:16])
 
 
 def iota(shape, dim):
@@ -118,6 +130,7 @@
         pay,
         recv,
         full,
+        scal,
         present,
         w_sum,
         w_dif,
@@ -127,6 +140,7 @@
         en_sem,
         rs_sem,
         ag_sem,
+        sc_sem,
         in_sem,
     ) = scratch
     (
@@ -321,7 +335,8 @@
     s_dir[...] = jnp.zeros(s_dir.shape, F32)
 
     row64 = iota((64, A), 0)
-    lane64 = iota((64, A), 1)
+    row16 = iota((16, A), 0)
+    lane1 = iota((1, A), 1)
 
     def lane_sum(v):
         return jnp.sum(v, axis=1, keepdims=True)
@@ -338,26 +353,25 @@
             top = full_f.astype(BF16)
             ff[pl.ds(k * 32, 32), :] = top
             ff[pl.ds(64 + k * 32, 32), :] = (full_f - top.astype(F32)).astype(BF16)
-        extra = jnp.zeros((64, A), F32)
+        extra = jnp.zeros((1, A), F32)
         for k in range(2):
             for j in range(4):
-                top = sums[j][k : k + 1].astype(BF16).astype(F32)
-                extra = jnp.where((row64 == k * 32 + 14) & (lane64 == j), top, extra)
-                extra = jnp.where((row64 == k * 32 + 15) & (lane64 == j), sums[j][k : k + 1] - top, extra)
+                extra = jnp.where(lane1 == 4 * k + j, sums[j][k : k + 1], extra)
+        scal[rnd, 0] = extra
         for j in range(3):
             s = dot_nt(ff[...], table[pl.ds(j * 256, 256), :])
             s = s[0:64] + s[64:128]
-            left = s[:, 0:128]
-            if j == 0:
-                left = left + extra
-            pay[rnd, pl.ds(8 * j, 4)] = left.astype(BF16).reshape(4, 16, A)
-            pay[rnd, pl.ds(8 * j + 4, 4)] = s[:, 128:256].astype(BF16).reshape(4, 16, A)
+            for t in range(8):
+                pay[rnd, 8 * j + t] = coded(s[(t % 4) * 16 : (t % 4) * 16 + 16, (t // 4) * A : (t // 4 + 1) * A])
 
         for k, (device, share, owns) in enumerate(peers):
 
             @pl.when(owns)
             def _():
                 remote(pay.at[rnd, share], recv.at[rnd, k], rs_sem.at[0, rnd], rs_sem.at[1, rnd], device).start()
+
+        for k, (device, _, _) in enumerate(peers):
+            remote(scal.at[rnd, 0], scal.at[rnd, k + 1], sc_sem.at[0, rnd], sc_sem.at[1, rnd], device).start()
 
         if rnd == 0:
             lax.fori_loop(H2, k_steps, count_triples, 0)
@@ -377,12 +391,10 @@
         @pl.when(grid.owner)
         def _():
             all_in(recv.at[rnd], rs_sem, rnd).wait_recv()
-            total = pay[rnd, grid.chunk].astype(F32)
+            total = decoded(pay[rnd, grid.chunk])
             for k in range(len(peers)):
-                total = total + recv[rnd, k].astype(F32)
-            scalar = total[14:15] + total[15:16]
-            top = scalar.astype(BF16).astype(F32)
-            full[rnd, grid.chunk] = jnp.concatenate([total[0:14], top, scalar - top], axis=0).astype(BF16)
+                total = total + decoded(recv[rnd, k])
+            full[rnd, grid.chunk] = coded(jnp.where(row16 < 14, total, 0.0))
             for device, _, _ in peers:
                 mine = full.at[rnd, grid.chunk]
                 remote(mine, mine, ag_sem.at[0, rnd], ag_sem.at[1, rnd], device).start()
@@ -392,11 +404,11 @@
         def _():
             all_in(full.at[rnd], ag_sem, rnd).wait_recv()
 
-        head = full[rnd, 0:4].reshape(64, A).astype(F32)
+        all_in(scal.at[rnd, pl.ds(0, len(peers))], sc_sem, rnd).wait_recv()
+        added = jnp.sum(scal[rnd], axis=0)
 
         def scalars(j):
-            both = [head[k + 14 : k + 15, j : j + 1] + head[k + 15 : k + 16, j : j + 1] for k in (0, 32)]
-            return jnp.concatenate(both, axis=0)
+            return jnp.concatenate([added[:, j : j + 1], added[:, 4 + j : 5 + j]], axis=0)
 
         norm, res_hard, cross, res_total = [scalars(j) for j in range(4)]
         if rnd == 0:
@@ -409,7 +421,7 @@
         beta_rows = jnp.where(row64 < 32, beta[0:1], beta[1:2])
         s_all = []
         for i in range(6):
-            s = full[rnd, pl.ds(i * 4, 4)].reshape(64, A).astype(F32)
+            s = jnp.concatenate([decoded(full[rnd, 4 * i + t]) for t in range(4)], axis=0)
             if rnd > 0:
                 s = s + beta_rows * s_dir[i]
             s_dir[i] = s
@@ -464,6 +476,7 @@
     pos_done.wait_send()
     en_done.wait_send()
     for rnd in range(ITERS):
+        all_in(scal.at[rnd, pl.ds(0, len(peers))], sc_sem, rnd).wait_send()
 
         @pl.when(grid.owner)
         def _():
@@ -516,9 +529,10 @@
                 pltpu.VMEM((2, atoms), F32),
                 pltpu.VMEM((2, atoms), F32),
                 pltpu.VMEM((2, atoms), F32),
-                pltpu.VMEM((ITERS, CHUNKS, 16, A), BF16),
-                pltpu.VMEM((ITERS, others, 16, A), BF16),
-                pltpu.VMEM((ITERS, CHUNKS, 16, A), BF16),
+                pltpu.VMEM((ITERS, CHUNKS, 16, A), jnp.int16),
+                pltpu.VMEM((ITERS, others, 16, A), jnp.int16),
+                pltpu.VMEM((ITERS, CHUNKS, 16, A), jnp.int16),
+                pltpu.VMEM((ITERS, others + 1, 1, A), F32),
                 pltpu.VMEM((32, HALF), F32),
                 pltpu.VMEM((3, 16, A), F32),
                 pltpu.VMEM((3, 16, A), F32),
@@ -526,6 +540,7 @@
                 pltpu.SemaphoreType.DMA((4,)),
                 pltpu.SemaphoreType.DMA((2,)),
                 pltpu.SemaphoreType.DMA((2,)),
+                pltpu.SemaphoreType.DMA((2, ITERS)),
                 pltpu.SemaphoreType.DMA((2, ITERS)),
                 pltpu.SemaphoreType.DMA((2, ITERS)),
                 pltpu.SemaphoreType.DMA((len(operands),)),

time: 69.5 us -> 70.5 us (1.014)
  Pallas kernels: 67.5 us -> 68.5 us
    pallas_call x1, Pallas kernels: 67.5 us -> 68.5 us  [local(): pl.pallas_call(functools.partial(kernel, sizes), out_shape=jax.ShapeDtype...]
where the time goes in v3:
time: 70.5 us; the launch traced here: 70.4 us
  Pallas kernels  68.5 us (97%)
  local copies, waits for them, and re-layouts  1.25 us (2%)
    pallas_call x1, Pallas kernels, local(): pl.pallas_call(functools.partial(kernel, sizes), out_shape=jax.ShapeDtype...  68.5 us

profile of v3, /device:TPU:1, one launch (start us, length us, event | category | flops | bytes accessed | tf_op | source)
XLA Modules:
  0.0 70.4 jit_solution(73636999935266886)
XLA Ops:
  0.6 68.5 %shard_map.149 = f32[2,128]{1,0:T(2,128)} custom-call(bf16[128,128]{1,0:T(8,128)(2,1)} %refs_0_.1, f32[3,128]{1,0:T(4,128)} %refs_1_.1, s32[1,128]{1,0:T(1,128)} %bitcast.11, s32[1,64]{1,0:T(1,128)} %refs_3_.1, s32[32,128]{1,0:T(8,128)} %bitcast.10, s32[1,128]{1,0:T(1,128)} %bitcast.12, s32[3,16384]{1,0:T(4,128)} %refs_6_.1, bf16[128,128]{1,0:T(8,128)(2,1)} %refs_7_.1, ...), custom_call_target="tpu_custom_call" | custom-call | tf_op jit(solution)/shard_map/pallas_call | solution.py:507
  69.1 1.3 %slice_bitcast_fusion = (f32[128]{0:T(128)}, f32[128]{0:T(128)}) fusion(f32[2,128]{1,0:T(2,128)} %shard_map.149), kind=kLoop, calls=%fused_computation | loop fusion | bytes 2048 | tf_op jit(solution)/shard_map/squeeze | solution.py:552

commit v4 on v3

--- a/solution.py
+++ b/solution.py
@@ -16,7 +16,7 @@
 A = 128
 NBR = 32
 HALF = 384
-CHUNKS = 24
+CHUNKS = 12
 TROWS = 160
 TURN = 2.0 * math.pi
 SIN_C = [(-1.0) ** k * TURN ** (2 * k + 1) / math.factorial(2 * k + 1) for k in range(10)]
@@ -78,21 +78,25 @@
         dom, x = lax.axis_index("dom"), lax.axis_index("kv")
         self.y, self.z, self.c, self.x = dom // (nz * nc), (dom // nc) % nz, dom % nc, x
         self.dom = dom
-        steps = [(dx, dy, dc) for dx in range(nx) for dy in range(ny) for dc in range(nc)]
-        steps.sort(key=lambda s: (-(ring(s[0], nx) + ring(s[1], ny)), s))
+        steps = [(dx, dy, dc) for dx in range(nx) for dy in range(2) for dc in range(nc)]
+        steps.sort(key=lambda s: (-(ring(s[0], nx) + s[1]), s))
         self.peers = []
         for dx, dy, dc in steps:
             if dx or dy or dc:
-                px, py, pc = (x + dx) % nx, (self.y + dy) % ny, (self.c + dc) % nc
+                px, py, pc = (x + dx) % nx, (self.y // 2) * 2 + (self.y + dy) % 2, (self.c + dc) % nc
                 self.peers.append(({"dom": (py * nz + self.z) * nc + pc, "kv": px}, *self.share(px, py, pc)))
         self.chunk, self.owner = self.share(x, self.y, self.c)
+        self.place = (self.y // 2) * nz + self.z
+        steps = sorted([(dz, dy) for dz in range(nz) for dy in range(2)], key=lambda s: (-(ring(s[0], nz) + s[1]), s))
         self.column = []
-        for dz in sorted(range(1, nz), key=lambda d: -ring(d, nz)):
-            self.column.append({"dom": (self.y * nz + (self.z + dz) % nz) * nc + self.c, "kv": x})
+        for dz, dy in steps:
+            if dz or dy:
+                py = self.y + dy * (ny - 1 - 2 * self.y)
+                self.column.append({"dom": (py * nz + (self.z + dz) % nz) * nc + self.c, "kv": x})
 
     def share(self, x, y, c):
         ny, nz, nc, nx = self.sizes
-        index = (y * nx + x) * nc + c
+        index = ((y % 2) * nx + x) * nc + c
         part = index % 4
         return (index // 4) * 3 + jnp.minimum(part, 2), part < 3
 
@@ -148,9 +152,9 @@
         w_upd_ref, w_out_ref, chi_ref, hard_ref,
     ) = arrived
     grid = Grid(sizes)
-    nz = sizes[1]
-    gid = grid.z
-    atoms = nz * A
+    gcount = 2 * sizes[1]
+    gid = grid.place
+    atoms = gcount * A
     peers, column = grid.peers, grid.column
     atoms_total = atoms * (len(peers) + 1)
     box_x = (atoms_total // A) * SLAB_W
@@ -236,7 +240,7 @@
     from_right, from_left = got[1].astype(F32), got[0].astype(F32)
     nbr_tab[:, A : 2 * A] = jnp.where(iota((TROWS, A), 1) < 32, from_right, from_left).astype(BF16)
 
-    group = 4
+    group = 16
     wide = group * A
     acc[...] = jnp.zeros(acc.shape, F32)
     own_pos = jnp.concatenate([pos] * group, axis=1)
@@ -274,7 +278,7 @@
             acc[c + 1] += fold(carried * unit[c : c + 1])
         return carry
 
-    lax.fori_loop(0, NBR // group, messages, 0)
+    lax.fori_loop(0, NBR // group, messages, 0, unroll=True)
     scale = 1.0 / math.sqrt(NBR)
     vec = [acc[c + 1] * scale for c in range(3)]
     vec_square = vec[0] * vec[0] + vec[1] * vec[1] + vec[2] * vec[2]
@@ -289,7 +293,7 @@
         remote(en_all.at[gid], en_all.at[gid], en_sem.at[0], en_sem.at[1], device).start()
 
     def gathered(ref, sem):
-        return remote(ref.at[pl.ds(0, nz - 1)], ref.at[pl.ds(0, nz - 1)], sem.at[0], sem.at[1], column[0])
+        return remote(ref.at[pl.ds(0, gcount - 1)], ref.at[pl.ds(0, gcount - 1)], sem.at[0], sem.at[1], column[0])
 
     pos_done = gathered(pos_all, pos_sem)
     pos_done.wait_recv()
@@ -317,7 +321,7 @@
         table[HALF : 2 * HALF, lanes] = jnp.concatenate(sin_rows, axis=0).astype(BF16)
         return carry
 
-    lax.fori_loop(0, nz, build, 0)
+    lax.fori_loop(0, gcount, build, 0)
     lax.fori_loop(H1, H2, count_triples, 0)
 
     en_done = gathered(en_all, en_sem)
@@ -329,7 +333,7 @@
         res[:, lanes] = jnp.where(iota((2, A), 0) == 0, -tile[0:2], 1.0)
         return carry
 
-    lax.fori_loop(0, nz, start_residual, 0)
+    lax.fori_loop(0, gcount, start_residual, 0)
     sol[...] = jnp.zeros(sol.shape, F32)
     direc[...] = jnp.zeros(direc.shape, F32)
     s_dir[...] = jnp.zeros(s_dir.shape, F32)
@@ -362,7 +366,7 @@
             s = dot_nt(ff[...], table[pl.ds(j * 256, 256), :])
             s = s[0:64] + s[64:128]
             for t in range(8):
-                pay[rnd, 8 * j + t] = coded(s[(t % 4) * 16 : (t % 4) * 16 + 16, (t // 4) * A : (t // 4 + 1) * A])
+                pay[rnd, 4 * j + t // 2, t % 2] = coded(s[(t % 4) * 16 : (t % 4) * 16 + 16, (t // 4) * A : (t // 4 + 1) * A])
 
         for k, (device, share, owns) in enumerate(peers):
 
@@ -391,10 +395,11 @@
         @pl.when(grid.owner)
         def _():
             all_in(recv.at[rnd], rs_sem, rnd).wait_recv()
-            total = decoded(pay[rnd, grid.chunk])
-            for k in range(len(peers)):
-                total = total + decoded(recv[rnd, k])
-            full[rnd, grid.chunk] = coded(jnp.where(row16 < 14, total, 0.0))
+            for t in range(2):
+                total = decoded(pay[rnd, grid.chunk, t])
+                for k in range(len(peers)):
+                    total = total + decoded(recv[rnd, k, t])
+                full[rnd, grid.chunk, t] = coded(jnp.where(row16 < 14, total, 0.0))
             for device, _, _ in peers:
                 mine = full.at[rnd, grid.chunk]
                 remote(mine, mine, ag_sem.at[0, rnd], ag_sem.at[1, rnd], device).start()
@@ -421,7 +426,7 @@
         beta_rows = jnp.where(row64 < 32, beta[0:1], beta[1:2])
         s_all = []
         for i in range(6):
-            s = jnp.concatenate([decoded(full[rnd, 4 * i + t]) for t in range(4)], axis=0)
+            s = jnp.concatenate([decoded(full[rnd, 2 * i + t // 2, t % 2]) for t in range(4)], axis=0)
             if rnd > 0:
                 s = s + beta_rows * s_dir[i]
             s_dir[i] = s
@@ -492,8 +497,9 @@
     sizes = (4, 8, 2, 4)
     ny, nz, nc, nx = sizes
     assert dict(mesh.shape) == {"dom": ny * nz * nc, "kv": nx}
-    atoms = nz * A
-    others = nx * ny * nc - 1
+    gcount = 2 * nz
+    atoms = gcount * A
+    others = nx * 2 * nc - 1
 
     def local(
         node_feats, positions, species, halo_rows, neighbours, nbr_count, recip_vectors,
@@ -514,8 +520,8 @@
                 pltpu.VMEM((TROWS, A), BF16),
                 pltpu.VMEM((TROWS, A), BF16),
                 pltpu.VMEM((2, TROWS, A), BF16),
-                pltpu.VMEM((nz, 8, A), F32),
-                pltpu.VMEM((nz, 8, A), F32),
+                pltpu.VMEM((gcount, 8, A), F32),
+                pltpu.VMEM((gcount, 8, A), F32),
                 pltpu.VMEM((TROWS, 2 * A), BF16),
                 pltpu.VMEM((NBR, A), I32),
                 pltpu.VMEM((4, A, A), F32),
@@ -529,9 +535,9 @@
                 pltpu.VMEM((2, atoms), F32),
                 pltpu.VMEM((2, atoms), F32),
                 pltpu.VMEM((2, atoms), F32),
-                pltpu.VMEM((ITERS, CHUNKS, 16, A), jnp.int16),
-                pltpu.VMEM((ITERS, others, 16, A), jnp.int16),
-                pltpu.VMEM((ITERS, CHUNKS, 16, A), jnp.int16),
+                pltpu.VMEM((ITERS, CHUNKS, 2, 16, A), jnp.int16),
+                pltpu.VMEM((ITERS, others, 2, 16, A), jnp.int16),
+                pltpu.VMEM((ITERS, CHUNKS, 2, 16, A), jnp.int16),
                 pltpu.VMEM((ITERS, others + 1, 1, A), F32),
                 pltpu.VMEM((32, HALF), F32),
                 pltpu.VMEM((3, 16, A), F32),

time: 70.5 us -> 65.4 us (0.928)
  Pallas kernels: 68.5 us -> 63.3 us
    pallas_call x1, Pallas kernels: 68.5 us -> 63.3 us  [local(): pl.pallas_call(functools.partial(kernel, sizes), out_shape=jax.ShapeDtype...]
where the time goes in v4:
time: 65.4 us; the launch traced here: 65.2 us
  Pallas kernels  63.3 us (97%)
  local copies, waits for them, and re-layouts  1.25 us (2%)
    pallas_call x1, Pallas kernels, local(): pl.pallas_call(functools.partial(kernel, sizes), out_shape=jax.ShapeDtype...  63.3 us

profile of v4, /device:TPU:1, one launch (start us, length us, event | category | flops | bytes accessed | tf_op | source)
XLA Modules:
  0.0 65.2 jit_solution(8440004505665140508)
XLA Ops:
  0.6 63.3 %shard_map.149 = f32[2,128]{1,0:T(2,128)} custom-call(bf16[128,128]{1,0:T(8,128)(2,1)} %refs_0_.1, f32[3,128]{1,0:T(4,128)} %refs_1_.1, s32[1,128]{1,0:T(1,128)} %bitcast.11, s32[1,64]{1,0:T(1,128)} %refs_3_.1, s32[32,128]{1,0:T(8,128)} %bitcast.10, s32[1,128]{1,0:T(1,128)} %bitcast.12, s32[3,16384]{1,0:T(4,128)} %refs_6_.1, bf16[128,128]{1,0:T(8,128)(2,1)} %refs_7_.1, ...), custom_call_target="tpu_custom_call" | custom-call | tf_op jit(solution)/shard_map/pallas_call | solution.py:513
  64.0 1.3 %slice_bitcast_fusion = (f32[128]{0:T(128)}, f32[128]{0:T(128)}) fusion(f32[2,128]{1,0:T(2,128)} %shard_map.149), kind=kLoop, calls=%fused_computation | loop fusion | bytes 2048 | tf_op jit(solution)/shard_map/squeeze | solution.py:558

commit v5 on v4

--- a/solution.py
+++ b/solution.py
@@ -136,9 +136,10 @@
         full,
         scal,
         present,
-        w_sum,
-        w_dif,
+        weights,
         s_dir,
+        ends,
+        ends_sent,
         halo_sem,
         pos_sem,
         en_sem,
@@ -161,12 +162,12 @@
     kvec = recip_ref.shape[1]
 
     loads = [pltpu.make_async_copy(src, dst, in_sem.at[i]) for i, (src, dst) in enumerate(zip(inputs, arrived))]
-    for i in (0, 7, 1, 3, 2, 13, 4, 5, 6, 8, 9, 10, 11, 12):
-        loads[i].start()
-
     barrier = pltpu.get_barrier_semaphore()
     partners = [grid.slab_peer(-1), grid.slab_peer(1)] + column + [device for device, _, _ in peers]
-    for device in partners:
+    for k, device in enumerate(partners):
+        if k == 2:
+            for i in (0, 7, 1, 3, 2, 13, 4, 5, 6, 8, 9, 10, 11, 12):
+                loads[i].start()
         pl.semaphore_signal(barrier, inc=1, device_id=device, device_id_type=MESH)
 
     def remote(src, dst, send, recv_, device):
@@ -317,8 +318,11 @@
             a, b = cz[j : j + 1], sz[j : j + 1]
             cos_rows.append(a * cy - b * sy)
             sin_rows.append(b * cy + a * sy)
-        table[0:HALF, lanes] = jnp.concatenate(cos_rows, axis=0).astype(BF16)
-        table[HALF : 2 * HALF, lanes] = jnp.concatenate(sin_rows, axis=0).astype(BF16)
+        cos_b = jnp.concatenate(cos_rows, axis=0).astype(BF16)
+        sin_b = jnp.concatenate(sin_rows, axis=0).astype(BF16)
+        for i in range(3):
+            table[2 * i * A : (2 * i + 1) * A, lanes] = cos_b[i * A : (i + 1) * A]
+            table[(2 * i + 1) * A : (2 * i + 2) * A, lanes] = sin_b[i * A : (i + 1) * A]
         return carry
 
     lax.fori_loop(0, gcount, build, 0)
@@ -338,7 +342,6 @@
     direc[...] = jnp.zeros(direc.shape, F32)
     s_dir[...] = jnp.zeros(s_dir.shape, F32)
 
-    row64 = iota((64, A), 0)
     row16 = iota((16, A), 0)
     lane1 = iota((1, A), 1)
 
@@ -348,7 +351,10 @@
     def all_in(ref, sem, rnd):
         return remote(ref, ref, sem.at[0, rnd], sem.at[1, rnd], column[0])
 
-    norm_old = dir_hard = dir_total = sol_total = None
+    def shared(rnd):
+        return full.at[rnd] if rnd + 1 < ITERS else ends
+
+    norm_old = energy = dir_hard = dir_total = sol_total = None
     for rnd in range(ITERS):
         r, p, h = res[...], direc[...], hard_all[...]
         sums = [lane_sum(r * r), lane_sum(h * r * r), lane_sum(h * r * p), lane_sum(r)]
@@ -363,10 +369,15 @@
                 extra = jnp.where(lane1 == 4 * k + j, sums[j][k : k + 1], extra)
         scal[rnd, 0] = extra
         for j in range(3):
-            s = dot_nt(ff[...], table[pl.ds(j * 256, 256), :])
+            s = dot_nt(table[pl.ds(j * 256, 256), :], ff[...]).T
             s = s[0:64] + s[64:128]
-            for t in range(8):
-                pay[rnd, 4 * j + t // 2, t % 2] = coded(s[(t % 4) * 16 : (t % 4) * 16 + 16, (t // 4) * A : (t // 4 + 1) * A])
+            for k in range(2):
+                cc, sc = s[k * 32 : k * 32 + 16, 0:A], s[k * 32 + 16 : k * 32 + 32, 0:A]
+                cs, ss = s[k * 32 : k * 32 + 16, A : 2 * A], s[k * 32 + 16 : k * 32 + 32, A : 2 * A]
+                pay[rnd, 2 * j + k, 0] = coded(cc - ss)
+                pay[rnd, 2 * j + k, 1] = coded(sc + cs)
+                pay[rnd, 6 + 2 * j + k, 0] = coded(cc + ss)
+                pay[rnd, 6 + 2 * j + k, 1] = coded(sc - cs)
 
         for k, (device, share, owns) in enumerate(peers):
 
@@ -389,25 +400,39 @@
             plus, minus = present[0:16] * weight, present[16:32] * weight
             for i in range(3):
                 lanes = slice(i * 128, (i + 1) * 128)
-                w_sum[i] = (plus + minus)[:, lanes]
-                w_dif[i] = (plus - minus)[:, lanes]
+                weights[i] = plus[:, lanes]
+                weights[3 + i] = minus[:, lanes]
 
         @pl.when(grid.owner)
         def _():
             all_in(recv.at[rnd], rs_sem, rnd).wait_recv()
+            parts = []
             for t in range(2):
                 total = decoded(pay[rnd, grid.chunk, t])
                 for k in range(len(peers)):
                     total = total + decoded(recv[rnd, k, t])
-                full[rnd, grid.chunk, t] = coded(jnp.where(row16 < 14, total, 0.0))
+                total = jnp.where(row16 < 14, total, 0.0)
+                if rnd + 1 < ITERS:
+                    full[rnd, grid.chunk, t] = coded(total)
+                parts.append(total)
+            if rnd + 1 < ITERS:
+                mine = full.at[rnd, grid.chunk]
+            else:
+                w = weights[grid.chunk // 2]
+                before = s_dir[grid.chunk]
+                square = w * (parts[0] * parts[0] + parts[1] * parts[1])
+                cross = w * (parts[0] * before[0:16] + parts[1] * before[16:32])
+                ends[grid.chunk] = jnp.concatenate(
+                    [jnp.sum(square, axis=0, keepdims=True), jnp.sum(cross, axis=0, keepdims=True)], axis=0
+                )
+                mine = ends.at[grid.chunk]
             for device, _, _ in peers:
-                mine = full.at[rnd, grid.chunk]
                 remote(mine, mine, ag_sem.at[0, rnd], ag_sem.at[1, rnd], device).start()
-            all_in(full.at[rnd, pl.ds(0, CHUNKS - 1)], ag_sem, rnd).wait_recv()
+            all_in(shared(rnd).at[pl.ds(0, CHUNKS - 1)], ag_sem, rnd).wait_recv()
 
         @pl.when(jnp.logical_not(grid.owner))
         def _():
-            all_in(full.at[rnd], ag_sem, rnd).wait_recv()
+            all_in(shared(rnd), ag_sem, rnd).wait_recv()
 
         all_in(scal.at[rnd, pl.ds(0, len(peers))], sc_sem, rnd).wait_recv()
         added = jnp.sum(scal[rnd], axis=0)
@@ -423,34 +448,23 @@
             beta = norm / norm_old
             dir_hard = res_hard + 2.0 * beta * cross + beta * beta * dir_hard
             dir_total = res_total + beta * dir_total
-        beta_rows = jnp.where(row64 < 32, beta[0:1], beta[1:2])
-        s_all = []
-        for i in range(6):
-            s = jnp.concatenate([decoded(full[rnd, 2 * i + t // 2, t % 2]) for t in range(4)], axis=0)
-            if rnd > 0:
-                s = s + beta_rows * s_dir[i]
-            s_dir[i] = s
-            s_all.append(s)
-        q_cos, q_sin = [], []
-        for i in range(3):
-            both, diff = w_sum[i], w_dif[i]
-            for k, out in ((0, q_cos), (1, q_sin)):
-                mine, other = s_all[3 * k + i], s_all[3 * (1 - k) + i]
-                sign = -1.0 if k == 0 else 1.0
-                parts = []
-                for rhs in (0, 32):
-                    for t in (0, 1):
-                        same = mine[rhs + 16 * t : rhs + 16 * t + 16]
-                        swap = other[rhs + 16 * (1 - t) : rhs + 16 * (1 - t) + 16]
-                        sign = -1.0 if t == k else 1.0
-                        parts.append(both * same + sign * (diff * swap))
-                out.append(jnp.concatenate(parts, axis=0))
-        q_all = q_cos + q_sin
-        energy = functools.reduce(jnp.add, [q * s for q, s in zip(q_all, s_all)])
-        energy = lane_sum(energy)
-        energy = jnp.concatenate(
-            [jnp.sum(energy[0:32], axis=0, keepdims=True), jnp.sum(energy[32:64], axis=0, keepdims=True)], axis=0
-        )
+        if rnd + 1 < ITERS:
+            q_all, energy = [], []
+            for o in range(CHUNKS):
+                s = jnp.concatenate([decoded(full[rnd, o, t]) for t in range(2)], axis=0)
+                if rnd > 0:
+                    s = s + beta[o % 2 : o % 2 + 1] * s_dir[o]
+                s_dir[o] = s
+                w = weights[o // 2]
+                q_all.append(jnp.concatenate([w, w], axis=0) * s)
+                energy.append(q_all[-1] * s)
+            energy = [jnp.sum(functools.reduce(jnp.add, energy[k::2]), axis=0, keepdims=True) for k in range(2)]
+            energy = lane_sum(jnp.concatenate(energy, axis=0))
+        else:
+            sums = [functools.reduce(jnp.add, [ends[o] for o in range(k, CHUNKS, 2)]) for k in range(2)]
+            square = lane_sum(jnp.concatenate([v[0:1] for v in sums], axis=0))
+            cross = lane_sum(jnp.concatenate([v[1:2] for v in sums], axis=0))
+            energy = square + 2.0 * beta * cross + beta * beta * energy
         alpha = norm / (dir_hard + energy)
         p = r + beta * p
         sol[...] += alpha * p
@@ -459,7 +473,16 @@
         norm_old = norm
         if rnd + 1 < ITERS:
             direc[...] = p
-            q_full = jnp.concatenate(q_all, axis=1)
+            tiles = []
+            for i in range(3):
+                cos_rows, sin_rows = [], []
+                for k in range(2):
+                    plus, minus = q_all[2 * i + k], q_all[6 + 2 * i + k]
+                    less = plus - minus
+                    cos_rows.append(plus + minus)
+                    sin_rows += [less[16:32], -less[0:16]]
+                tiles += [jnp.concatenate(cos_rows, axis=0), jnp.concatenate(sin_rows, axis=0)]
+            q_full = jnp.concatenate(tiles, axis=1)
             top = q_full.astype(BF16)
             qq = jnp.concatenate([top, (q_full - top.astype(F32)).astype(BF16)], axis=0)
             piece = 512 if atoms % 512 == 0 else atoms
@@ -486,7 +509,8 @@
         @pl.when(grid.owner)
         def _():
             all_in(pay.at[rnd, pl.ds(0, CHUNKS - 1)], rs_sem, rnd).wait_send()
-            all_in(recv.at[rnd], ag_sem, rnd).wait_send()
+            sent = recv.at[rnd] if rnd + 1 < ITERS else ends_sent
+            all_in(sent, ag_sem, rnd).wait_send()
 
         @pl.when(jnp.logical_not(grid.owner))
         def _():
@@ -540,9 +564,10 @@
                 pltpu.VMEM((ITERS, CHUNKS, 2, 16, A), jnp.int16),
                 pltpu.VMEM((ITERS, others + 1, 1, A), F32),
                 pltpu.VMEM((32, HALF), F32),
-                pltpu.VMEM((3, 16, A), F32),
-                pltpu.VMEM((3, 16, A), F32),
-                pltpu.VMEM((6, 64, A), F32),
+                pltpu.VMEM((6, 16, A), F32),
+                pltpu.VMEM((CHUNKS, 32, A), F32),
+                pltpu.VMEM((CHUNKS, 2, A), F32),
+                pltpu.VMEM((others, 2, A), F32),
                 pltpu.SemaphoreType.DMA((4,)),
                 pltpu.SemaphoreType.DMA((2,)),
                 pltpu.SemaphoreType.DMA((2,)),

time: 65.4 us -> 64.9 us (level)
  no operation moved by 1% of the time
where the time goes in v5:
time: 64.9 us; the launch traced here: 64.7 us
  Pallas kernels  62.8 us (97%)
  local copies, waits for them, and re-layouts  1.25 us (2%)
    pallas_call x1, Pallas kernels, local(): pl.pallas_call(functools.partial(kernel, sizes), out_shape=jax.ShapeDtype...  62.8 us

profile of v5, /device:TPU:1, one launch (start us, length us, event | category | flops | bytes accessed | tf_op | source)
XLA Modules:
  0.0 64.7 jit_solution(9305098521291605056)
XLA Ops:
  0.6 62.8 %shard_map.149 = f32[2,128]{1,0:T(2,128)} custom-call(bf16[128,128]{1,0:T(8,128)(2,1)} %refs_0_.1, f32[3,128]{1,0:T(4,128)} %refs_1_.1, s32[1,128]{1,0:T(1,128)} %bitcast.11, s32[1,64]{1,0:T(1,128)} %refs_3_.1, s32[32,128]{1,0:T(8,128)} %bitcast.10, s32[1,128]{1,0:T(1,128)} %bitcast.12, s32[3,16384]{1,0:T(4,128)} %refs_6_.1, bf16[128,128]{1,0:T(8,128)(2,1)} %refs_7_.1, ...), custom_call_target="tpu_custom_call" | custom-call | tf_op jit(solution)/shard_map/pallas_call | solution.py:537
  63.5 1.3 %slice_bitcast_fusion = (f32[128]{0:T(128)}, f32[128]{0:T(128)}) fusion(f32[2,128]{1,0:T(2,128)} %shard_map.149), kind=kLoop, calls=%fused_computation | loop fusion | bytes 2048 | tf_op jit(solution)/shard_map/squeeze | solution.py:583

commit v6 on v5

--- a/solution.py
+++ b/solution.py
@@ -241,7 +241,7 @@
     from_right, from_left = got[1].astype(F32), got[0].astype(F32)
     nbr_tab[:, A : 2 * A] = jnp.where(iota((TROWS, A), 1) < 32, from_right, from_left).astype(BF16)
 
-    group = 16
+    group = 32
     wide = group * A
     acc[...] = jnp.zeros(acc.shape, F32)
     own_pos = jnp.concatenate([pos] * group, axis=1)
@@ -369,8 +369,8 @@
                 extra = jnp.where(lane1 == 4 * k + j, sums[j][k : k + 1], extra)
         scal[rnd, 0] = extra
         for j in range(3):
-            s = dot_nt(table[pl.ds(j * 256, 256), :], ff[...]).T
-            s = s[0:64] + s[64:128]
+            tiles = [dot_nt(table[pl.ds(j * 256 + t * A, A), :], ff[...]).T for t in range(2)]
+            s = jnp.concatenate([tile[0:64] + tile[64:128] for tile in tiles], axis=1)
             for k in range(2):
                 cc, sc = s[k * 32 : k * 32 + 16, 0:A], s[k * 32 + 16 : k * 32 + 32, 0:A]
                 cs, ss = s[k * 32 : k * 32 + 16, A : 2 * A], s[k * 32 + 16 : k * 32 + 32, A : 2 * A]

time: 64.9 us -> 63.4 us (0.977)
  Pallas kernels: 62.8 us -> 61.4 us
    pallas_call x1, Pallas kernels: 62.8 us -> 61.4 us  [local(): pl.pallas_call(functools.partial(kernel, sizes), out_shape=jax.ShapeDtype...]
where the time goes in v6:
time: 63.4 us; the launch traced here: 63.3 us
  Pallas kernels  61.4 us (97%)
  local copies, waits for them, and re-layouts  1.25 us (2%)
  between operations  0.64 us (1%)
    pallas_call x1, Pallas kernels, local(): pl.pallas_call(functools.partial(kernel, sizes), out_shape=jax.ShapeDtype...  61.4 us

profile of v6, /device:TPU:1, one launch (start us, length us, event | category | flops | bytes accessed | tf_op | source)
XLA Modules:
  0.0 63.3 jit_solution(14839909876155080845)
XLA Ops:
  0.6 61.4 %shard_map.149 = f32[2,128]{1,0:T(2,128)} custom-call(bf16[128,128]{1,0:T(8,128)(2,1)} %refs_0_.1, f32[3,128]{1,0:T(4,128)} %refs_1_.1, s32[1,128]{1,0:T(1,128)} %bitcast.11, s32[1,64]{1,0:T(1,128)} %refs_3_.1, s32[32,128]{1,0:T(8,128)} %bitcast.10, s32[1,128]{1,0:T(1,128)} %bitcast.12, s32[3,16384]{1,0:T(4,128)} %refs_6_.1, bf16[128,128]{1,0:T(8,128)(2,1)} %refs_7_.1, ...), custom_call_target="tpu_custom_call" | custom-call | tf_op jit(solution)/shard_map/pallas_call | solution.py:537
  62.0 1.3 %slice_bitcast_fusion = (f32[128]{0:T(128)}, f32[128]{0:T(128)}) fusion(f32[2,128]{1,0:T(2,128)} %shard_map.149), kind=kLoop, calls=%fused_computation | loop fusion | bytes 2048 | tf_op jit(solution)/shard_map/squeeze | solution.py:583
